TPU v7x, 256 devices: a whole 4x4x8 slice. The times are simulated.
256 devices in a mesh: gx: 32 (over y, z), gy: 8 (over x, core).
Axes of the slice: x: 4, y: 4, z: 8, core: 2. Of those that a mesh axis runs over, the one named last changes fastest.
Arguments:
- dual_ops: bfloat16 [128, 32, 512, 512], P('gx', 'gy'), may hold values from -2 to 8, as said below
- dual_load: float32 [128, 32, 2, 128], P('gx', 'gy'), may hold values from -100 to 100
- mode_images: float32 [128, 32, 3, 512], P('gx', 'gy'), may hold values from -0.25 to 0.25
- mode_loads: float32 [128, 32, 3], P('gx', 'gy'), may hold values from -24 to 24
- coarse_factor: float32 [12288, 12288], P(('gx', 'gy')), may hold values from -1 to 2
- west_map: int32 [128, 32, 128], P('gx', 'gy'), may hold values from 0 to 127, each once within a row
- south_map: int32 [128, 32, 128], P('gx', 'gy'), may hold values from 0 to 127, each once within a row
- mode_owner: int32 [12288], P(('gx', 'gy')), may hold values from 0 to 47, as said below
Outputs:
- multipliers: float32 [128, 32, 2, 128], P('gx', 'gy')
- projected_gradient: float32 [128, 32, 2, 128], P('gx', 'gy')
- amplitudes: float32 [128, 32, 3], P('gx', 'gy')
Inputs may be any that keep to these rules, and one draw needn't show every extreme that they name: west_map[x, y] is a permutation: entry j is the index, within the east side of subdomain (x - 1, y), of the multiplier at position j of the west side of subdomain (x, y). south_map[x, y] is a permutation: entry j is the index, within the north side of subdomain (x, y - 1), of the multiplier at position j of the south side of subdomain (x, y). `mode_owner`: each aligned block of 48 entries is a permutation. dual_ops(x, y) is symmetric.
All inputs are finite; a program needn't handle non-finite values.
Results may differ from a plain program's by a relative error of at most 0.0011.
Values sent between devices are 32-bit elements; how exact they have to be, the bound alone decides.
No kernel may reach another device: no remote copies, remote signals or barrier semaphores. Data moves between devices by JAX's collectives and lax.ppermute only.
A program may use at most 64 MiB of HBM per device.

v0:
```python
import jax
import jax.numpy as jnp
from jax import lax
from jax.experimental import pallas as pl
from jax.experimental.pallas import tpu as pltpu
from jax.sharding import PartitionSpec as P

GX, GY = "gx", "gy"
ALL = (GX, GY)
SUB = 16
E = 128
MODES = 3
BLOCK = 48
PEERS = 256
LANES = 128

AT_W, AT_E, AT_S, AT_N, AT_SCALAR = 48, 60, 72, 84, 96


def lane_gather(values, index):
    return jnp.take_along_axis(values, index, axis=1)


def up(values, rows):
    return pltpu.roll(values, values.shape[0] - rows, 0)


def down(values, rows):
    return pltpu.roll(values, rows, 0)


class Local:
    def __init__(self, refs):
        self.refs = refs
        s = lax.broadcasted_iota(jnp.int32, (SUB, LANES), 0)
        self.lane = lax.broadcasted_iota(jnp.int32, (SUB, LANES), 1)
        x = lax.shift_right_logical(s, 2)
        y = lax.bitwise_and(s, 3)
        self.x, self.y, self.s = x, y, s

    def own_at(self, r):
        return 3 * self.s + r

    def west_at(self, r):
        return AT_W + 3 * self.y + r

    def east_at(self, r):
        return AT_E + 3 * self.y + r

    def south_at(self, r):
        return AT_S + 3 * self.x + r

    def north_at(self, r):
        return AT_N + 3 * self.x + r

    def cross(self, w, t, nb):
        x, y = self.x, self.y
        nb_tw, nb_we, nb_ts, nb_wn = nb
        keep_w, keep_s, wmap, smap = (self.refs[k][...] for k in ("kw", "ks", "wmap", "smap"))
        east = w[1] - up(jnp.where(x == 0, nb_tw, t[0]), 4)
        north = w[3] - jnp.where(y == 3, down(nb_ts, 3), up(t[1], 1))
        from_west = down(jnp.where(x == 3, nb_we, w[1]), 4)
        from_south = jnp.where(y == 0, up(nb_wn, 3), down(w[3], 1))
        west = keep_w * (w[0] - lane_gather(from_west, wmap))
        south = keep_s * (w[2] - lane_gather(from_south, smap))
        return west, east, south, north

    def modes(self, r, side):
        return self.refs["m"][r, :, side * E : (side + 1) * E]

    def lift(self, row):
        a = jnp.broadcast_to(row, (SUB, LANES))
        refs = self.refs
        w = [0.0] * 4
        t = [0.0] * 2
        nb = [0.0] * 4
        for r in range(MODES):
            own = lane_gather(a, self.own_at(r))
            for side in range(4):
                w[side] += self.modes(r, side) * own
            t[0] += refs["tmw"][r] * own
            t[1] += refs["tms"][r] * own
            nb[0] += refs["nb_tmw"][r] * lane_gather(a, self.east_at(r))
            nb[1] += refs["nb_me"][r] * lane_gather(a, self.west_at(r))
            nb[2] += refs["nb_tms"][r] * lane_gather(a, self.north_at(r))
            nb[3] += refs["nb_mn"][r] * lane_gather(a, self.south_at(r))
        return self.cross(w, t, nb)

    def put(self, total, values, at, rows=None):
        here = self.lane == at
        if rows is not None:
            here = here & rows
        return total + jnp.where(here, jnp.sum(values, axis=1, keepdims=True), 0.0)

    def absorb(self, total, u):
        for r in range(MODES):
            terms = sum(self.modes(r, side) * u[side] for side in range(4))
            total = self.put(total, terms, self.own_at(r))
        return total

    def contributions(self, w, t):
        refs, x, y = self.refs, self.x, self.y
        none = jnp.zeros((SUB, LANES), jnp.float32)
        total = self.absorb(none, self.cross(w, t, (none, none, none, none)))
        to_e, to_w = down(w[1], 4), up(t[0], 4)
        to_n, to_s = up(w[3], 3), down(t[1], 3)
        for r in range(MODES):
            total = self.put(total, -refs["nb_tmw"][r] * to_e, self.east_at(r), x == 0)
            total = self.put(total, -refs["nb_me"][r] * to_w, self.west_at(r), x == 3)
            total = self.put(total, -refs["nb_tms"][r] * to_n, self.north_at(r), y == 0)
            total = self.put(total, -refs["nb_mn"][r] * to_s, self.south_at(r), y == 3)
        return total

    def dual(self, u, precise):
        ops = self.refs["ops"]
        whole = jnp.concatenate(u, axis=1)
        left = whole.astype(jnp.bfloat16)
        if precise:
            rest = (whole - left.astype(jnp.float32)).astype(jnp.bfloat16)
            left = jnp.concatenate([left, rest], axis=0)
        row = lax.broadcasted_iota(jnp.int32, (SUB, 4 * E), 0)
        out = jnp.zeros((SUB, 4 * E), jnp.float32)
        for k in range(SUB):
            product = jnp.dot(left, ops[k], preferred_element_type=jnp.float32)
            if precise:
                product = product[:SUB] + product[SUB:]
            out = jnp.where(row == k, product, out)
        w = [out[:, side * E : (side + 1) * E] for side in range(4)]
        t = lane_gather(w[0], self.refs["winv"][...]), lane_gather(w[2], self.refs["sinv"][...])
        return w, t

    def send(self, total, ref):
        ref[...] = jnp.broadcast_to(jnp.sum(total, axis=0, keepdims=True), ref.shape)


def from_peers(ref):
    return jnp.sum(ref[...], axis=0, keepdims=True)


def scalar(ref, i):
    return ref[0:1, AT_SCALAR + i : AT_SCALAR + i + 1]


def keep(ref, parts):
    for i, part in enumerate(parts):
        ref[i] = part


def sides(ref):
    return [ref[i] for i in range(ref.shape[0])]


SETUP = ("kw", "ks", "wmap", "smap", "winv", "sinv", "m", "tmw", "tms", "nb_tmw", "nb_me", "nb_tms", "nb_mn")


def setup_kernel(wmap_t, smap_t, m, winv, sinv, tmw, tms):
    lane = lax.broadcasted_iota(jnp.int32, (E, E), 1)
    at = lax.broadcasted_iota(jnp.int32, (E, E), 0).astype(jnp.float32)
    for source, inverse in ((wmap_t, winv), (smap_t, sinv)):
        rows = []
        for k in range(SUB):
            hit = source[:, k : k + 1] == lane
            rows.append(jnp.sum(jnp.where(hit, at, 0.0), axis=0, keepdims=True))
        inverse[...] = jnp.concatenate(rows, axis=0).astype(jnp.int32)
    for r in range(MODES):
        tmw[r] = lane_gather(m[r, :, 0:E], winv[...])
        tms[r] = lane_gather(m[r, :, 2 * E : 3 * E], sinv[...])


def first_kernel(*refs):
    n = len(SETUP)
    local = Local(dict(zip(SETUP, refs[:n])))
    arrived, ops, load_e, load_n, nb_load_e, nb_load_n = refs[n : n + 6]
    out_row, lam, target, w_out, t_out = refs[n + 6 :]
    local.refs["ops"] = ops
    u = local.lift(from_peers(arrived))
    w, t = local.dual(u, False)
    none = jnp.zeros((SUB, LANES), jnp.float32)
    load = local.cross(
        (none, load_e[...], none, load_n[...]), (none, none), (none, nb_load_e[...], none, nb_load_n[...])
    )
    local.send(local.absorb(-local.contributions(w, t), load), out_row)
    keep(lam, (u[1], u[3]))
    keep(target, load)
    keep(w_out, w)
    keep(t_out, t)


def second_kernel(*refs):
    n = len(SETUP)
    local = Local(dict(zip(SETUP, refs[:n])))
    arrived, ops, target, w_in, t_in, nb0, nb1, nb2, nb3 = refs[n : n + 9]
    out_row, coarse, gradient, w_out, t_out = refs[n + 9 :]
    local.refs["ops"] = ops
    row = from_peers(arrived)
    image = local.cross(sides(w_in), sides(t_in), (nb0[...], nb1[...], nb2[...], nb3[...]))
    lifted = local.lift(row)
    g = [target[i] - image[i] - lifted[i] for i in range(4)]
    w, t = local.dual(g, False)
    total = local.contributions(w, t)
    total = local.put(total, g[1] * g[1] + g[3] * g[3], AT_SCALAR)
    total = local.put(total, sum(g[i] * w[i] for i in range(4)), AT_SCALAR + 1)
    local.send(total, out_row)
    coarse[...] = row
    keep(gradient, g)
    keep(w_out, w)
    keep(t_out, t)


def third_kernel(*refs):
    n = len(SETUP)
    local = Local(dict(zip(SETUP, refs[:n])))
    arrived, ops, sums, lam, coarse, gradient, w_in, t_in, nb0, nb1, nb2, nb3 = refs[n : n + 12]
    out_row, lam_out, coarse_out, moved, projected, g_out, w_out, t_out = refs[n + 12 :]
    local.refs["ops"] = ops
    alpha = scalar(sums, 0) / scalar(sums, 1)
    row = from_peers(arrived)
    w1 = sides(w_in)
    image = local.cross(w1, sides(t_in), (nb0[...], nb1[...], nb2[...], nb3[...]))
    lifted = local.lift(row)
    p = [image[i] - lifted[i] for i in range(4)]
    g0 = sides(gradient)
    g = [g0[i] - alpha * p[i] for i in range(4)]
    w, t = local.dual(g, True)
    total = local.contributions(w, t)
    total = local.put(total, g[1] * g[1] + g[3] * g[3], AT_SCALAR)
    total = local.put(total, sum(g[i] * w[i] for i in range(4)), AT_SCALAR + 1)
    total = local.put(total, sum(g0[i] * w[i] + g[i] * w1[i] for i in range(4)), AT_SCALAR + 2)
    local.send(total, out_row)
    keep(lam_out, (lam[0] + alpha * g0[1], lam[1] + alpha * g0[3]))
    coarse_out[...] = coarse[...] - alpha * row
    moved[...] = row
    keep(projected, (p[1], p[3]))
    keep(g_out, (g[1], g[3]))
    keep(w_out, w)
    keep(t_out, t)


def last_kernel(*refs):
    n = len(SETUP)
    local = Local(dict(zip(SETUP, refs[:n])))
    (arrived, sums, sums_next, lam, coarse, moved, g0, projected, g1, w_in, t_in, nb0, nb1, nb2, nb3) = refs[n : n + 15]
    lam_out, g_out, amplitudes = refs[n + 15 :]
    beta = scalar(sums_next, 0) / scalar(sums, 0)
    curve = scalar(sums_next, 1) + beta * (scalar(sums_next, 2) + beta * scalar(sums, 1))
    alpha = scalar(sums_next, 0) / curve
    row = from_peers(arrived)
    image = local.cross(sides(w_in), sides(t_in), (nb0[...], nb1[...], nb2[...], nb3[...]))
    lifted = local.lift(row)
    for i, side in ((0, 1), (1, 3)):
        p = image[side] - lifted[side] + beta * projected[i]
        g_out[i] = g1[i] - alpha * p
        lam_out[i] = lam[i] + alpha * (g1[i] + beta * g0[side])
    amplitudes[...] = alpha * (row + beta * moved[...]) - coarse[...]


def coarse_body(entries, owner, inverse, factor, out, first):
    lane = lax.broadcasted_iota(jnp.int32, (PEERS, LANES), 1)
    group = (
        (lane >= 12).astype(jnp.int32) + (lane >= 24).astype(jnp.int32) + (lane >= 36).astype(jnp.int32)
    )
    within = lane - 12 * group
    if first:
        total = entries
    else:
        from_e = up(lane_gather(entries, jnp.minimum(lane + 12, 127)), 8)
        from_w = down(lane_gather(entries, jnp.minimum(lane + 60, 127)), 8)
        from_n = up(lane_gather(entries, jnp.clip(63 + 3 * group + within, 0, 127)), 1)
        from_s = down(lane_gather(entries, jnp.clip(84 + 3 * group + within, 0, 127)), 1)
        total = entries + jnp.where(lane >= 36, from_e, 0.0) + jnp.where(lane < 12, from_w, 0.0)
        total = total + jnp.where(within >= 9, from_n, 0.0) + jnp.where(within < 3, from_s, 0.0)
    flat = lane_gather(total, owner)
    half = PEERS // 2
    low = lax.broadcasted_iota(jnp.int32, (half, LANES), 1) < 64
    e = jnp.where(low, flat[:half], pltpu.roll(flat[half:], 64, 1))
    z = jnp.zeros((half, LANES), jnp.float32)
    for k in range(BLOCK):
        z = z + factor[k] * jnp.sum(factor[k] * e)
    spread = jnp.concatenate([z, pltpu.roll(z, 64, 1)], axis=0)
    natural = lane_gather(spread, inverse)
    third = lane - AT_S
    g3 = jnp.zeros_like(lane)
    for c in (3, 6, 9):
        g3 = g3 + (third >= c).astype(jnp.int32)
    fourth = lane - AT_N
    g4 = jnp.zeros_like(lane)
    for c in (3, 6, 9):
        g4 = g4 + (fourth >= c).astype(jnp.int32)
    clip = lambda index: jnp.clip(index, 0, 127)
    at_w = down(lane_gather(natural, clip(lane - 12)), 8)
    at_e = up(lane_gather(natural, clip(lane - 60)), 8)
    at_s = down(lane_gather(natural, clip(9 * g3 + 9 + third)), 1)
    at_n = up(lane_gather(natural, clip(9 * g4 + fourth)), 1)
    edge = jnp.where(lane < AT_E, at_w, jnp.where(lane < AT_S, at_e, jnp.where(lane < AT_N, at_s, at_n)))
    out[...] = jnp.where(lane < AT_W, natural, edge)


def coarse_first_kernel(entries, factor, out, owner_out, inverse_out):
    lane = lax.broadcasted_iota(jnp.int32, (PEERS, LANES), 1)
    got = entries[...]
    owner = pltpu.roll(got, LANES - BLOCK, 1).astype(jnp.int32)
    owner = jnp.where(lane < BLOCK, owner, lane)
    inverse = lane
    for j in range(BLOCK):
        inverse = jnp.where(owner[:, j : j + 1] == lane, j, inverse)
    owner_out[...] = owner
    inverse_out[...] = inverse
    coarse_body(got, owner, inverse, factor, out, True)


def coarse_kernel(entries, owner, inverse, factor, out, sums):
    got = entries[...]
    sums[...] = jnp.sum(got, axis=0, keepdims=True)
    coarse_body(got, owner[...], inverse[...], factor, out, False)


def f32(*shape):
    return jax.ShapeDtypeStruct(shape, jnp.float32)


def i32(*shape):
    return jax.ShapeDtypeStruct(shape, jnp.int32)


def call(kernel, outs, *args):
    return pl.pallas_call(
        kernel,
        out_shape=outs,
        in_specs=[pl.BlockSpec(memory_space=pltpu.VMEM)] * len(args),
        out_specs=tuple(pl.BlockSpec(memory_space=pltpu.VMEM) for _ in outs),
        compiler_params=pltpu.CompilerParams(vmem_limit_bytes=40 * 1024 * 1024),
    )(*args)


def exchange(rows):
    return lax.all_to_all(rows, ALL, split_axis=0, concat_axis=0, tiled=True)


def from_next(value, axis):
    n = lax.axis_size(axis)
    return lax.ppermute(value, axis, [(i + 1, i) for i in range(n - 1)])


def from_previous(value, axis):
    n = lax.axis_size(axis)
    return lax.ppermute(value, axis, [(i, i + 1) for i in range(n - 1)])


def halo(w, t):
    return from_next(t[0], GX), from_previous(w[1], GX), from_next(t[1], GY), from_previous(w[3], GY)


def shards(dual_ops, dual_load, mode_images, mode_loads, coarse_factor, west_map, south_map, mode_owner):
    row = jnp.concatenate([mode_loads.reshape(BLOCK), mode_owner.astype(jnp.float32), jnp.zeros(32, jnp.float32)])
    arrived = exchange(jnp.broadcast_to(row[None], (PEERS, LANES)))

    ops = dual_ops.reshape(SUB, 4 * E, 4 * E)
    wmap, smap = west_map.reshape(SUB, E), south_map.reshape(SUB, E)
    m = mode_images.reshape(SUB, MODES, 4 * E).transpose(1, 0, 2)
    load = dual_load.reshape(SUB, 2, E)
    load_e, load_n = load[:, 0], load[:, 1]
    s = lax.broadcasted_iota(jnp.int32, (SUB, LANES), 0)
    kw = jnp.where((lax.axis_index(GX) == 0) & (s < 4), 0.0, 1.0).astype(jnp.float32)
    ks = jnp.where((lax.axis_index(GY) == 0) & (s % 4 == 0), 0.0, 1.0).astype(jnp.float32)
    winv, sinv, tmw, tms = call(
        setup_kernel,
        (i32(SUB, E), i32(SUB, E), f32(MODES, SUB, E), f32(MODES, SUB, E)),
        wmap.T,
        smap.T,
        m,
    )
    nb_tmw, nb_tms = from_next(tmw, GX), from_next(tms, GY)
    nb_e = from_previous(jnp.concatenate([m[:, :, E : 2 * E], load_e[None]], axis=0), GX)
    nb_n = from_previous(jnp.concatenate([m[:, :, 3 * E :], load_n[None]], axis=0), GY)
    setup = (kw, ks, wmap, smap, winv, sinv, m, tmw, tms, nb_tmw, nb_e[:3], nb_tms, nb_n[:3])
    blocks = coarse_factor.reshape(BLOCK, 2, PEERS // 2, BLOCK)
    blocks = jnp.pad(blocks, ((0, 0), (0, 0), (0, 0), (0, 16)))
    factor = jnp.concatenate([blocks[:, 0], blocks[:, 1]], axis=-1)

    rows_out = f32(PEERS, LANES)
    row_out = f32(1, LANES)
    four, two = f32(4, SUB, E), f32(2, SUB, E)

    partial, owner, inverse = call(
        coarse_first_kernel, (rows_out, i32(PEERS, LANES), i32(PEERS, LANES)), arrived, factor
    )
    out_row, lam, target, w, t = call(
        first_kernel,
        (rows_out, two, four, four, two),
        *setup,
        exchange(partial),
        ops,
        load_e,
        load_n,
        nb_e[3],
        nb_n[3],
    )
    near = halo(w, t)
    partial, _ = call(coarse_kernel, (rows_out, row_out), exchange(out_row), owner, inverse, factor)
    out_row, coarse, g0, w1, t1 = call(
        second_kernel, (rows_out, row_out, four, four, two), *setup, exchange(partial), ops, target, w, t, *near
    )
    near = halo(w1, t1)
    partial, sums = call(coarse_kernel, (rows_out, row_out), exchange(out_row), owner, inverse, factor)
    out_row, lam, coarse, moved, projected, g1, w2, t2 = call(
        third_kernel,
        (rows_out, two, row_out, row_out, two, two, four, two),
        *setup,
        exchange(partial),
        ops,
        sums,
        lam,
        coarse,
        g0,
        w1,
        t1,
        *near,
    )
    near = halo(w2, t2)
    partial, sums_next = call(coarse_kernel, (rows_out, row_out), exchange(out_row), owner, inverse, factor)
    lam, g, amplitudes = call(
        last_kernel,
        (two, two, row_out),
        *setup,
        exchange(partial),
        sums,
        sums_next,
        lam,
        coarse,
        moved,
        g0,
        projected,
        g1,
        w2,
        t2,
        *near,
    )

    def owned(value):
        return value.transpose(1, 0, 2).reshape(4, 4, 2, E)

    return owned(lam), owned(g), amplitudes[0, :BLOCK].reshape(4, 4, MODES)


def solution(mesh):
    placed = (
        P(GX, GY, None, None),
        P(GX, GY, None, None),
        P(GX, GY, None, None),
        P(GX, GY, None),
        P(ALL, None),
        P(GX, GY, None),
        P(GX, GY, None),
        P(ALL),
    )
    return jax.shard_map(
        shards,
        mesh=mesh,
        in_specs=placed,
        out_specs=(P(GX, GY, None, None), P(GX, GY, None, None), P(GX, GY, None)),
        check_vma=False,
    )
```

profile of v0, /device:TPU:30, one launch (start us, length us, event | category | flops | bytes accessed | tf_op | source)
XLA Modules:
  0.0 291.4 jit_solution(12680587768724721681)
XLA Ops:
  0.6 0.9 copy.28
  1.6 0.8 copy.29.wmap_t
  3.2 1.4 shard_map.103
  5.7 7.9 %collective-permute-start = (f32[3,16,128]{2,1,0:T(8,128)}, f32[3,16,128]{2,1,0:T(8,128)}, u32[]{:S(2)}, u32[]{:S(2)}) collective-permute-start(f32[3,16,128]{2,1,0:T(8,128)} %get-tuple-element.38.refs_7_), channel_id=1, source_target_pairs={{8,0},{16,8},{24,16},{32,24},{40,32},{48,40},{56,48},{64,56},{72,6... | collective-permute-start | bytes 73736 | tf_op jit(solution)/shard_map/ppermute | solution.py:341
  13.7 1.9 collective-permute-start.2
  17.6 1.9 collective-permute-start.1
  20.1 3.0 %collective-permute-start.3 = (f32[4,16,128]{2,1,0:T(8,128)}, f32[4,16,128]{2,1,0:T(8,128)S(1)}, u32[]{:S(2)}, u32[]{:S(2)}) collective-permute-start(f32[4,16,128]{2,1,0:T(8,128)} %pad_maximum_fusion.2), channel_id=1, source_target_pairs={{0,1},{1,2},{2,3},{3,4},{4,5},{5,6},{6,7},{8,9},{9,10},{10,11},{11... | collective-permute-start | bytes 98312 | tf_op jit(solution)/shard_map/ppermute | solution.py:346
  23.1 0.8 copy.32
  25.5 11.0 %all-to-all-start = ((f32[256,1,128]{2,1,0:T(1,128)}), f32[256,1,128]{2,1,0:T(1,128)S(1)}, u32[]{:S(2)}, u32[]{:S(2)}) async-start(f32[256,1,128]{2,1,0:T(1,128)} %broadcast_in_dim.28), calls=%async_computation | async-start | bytes 262144 | tf_op jit(solution)/shard_map/all_to_all | solution.py:336
  36.5 5.9 %reshape.58 = f32[48,2,128,48]{3,2,1,0:T(8,128)} reshape(f32[48,12288]{1,0:T(8,128)} %param.12) | data formatting | bytes 4718592 | tf_op jit(solution)/shard_map/reshape | solution.py:376
  42.4 6.6 %fusion = (f32[48,128,64]{2,1,0:T(8,128)}, f32[48,128,64]{2,1,0:T(8,128)}) fusion(f32[48,2,128,48]{3,2,1,0:T(8,128)} %reshape.58), kind=kLoop, calls=%fused_computation.2 | loop fusion | bytes 5505024 | tf_op jit(solution)/shard_map/squeeze | solution.py:378
  49.7 3.7 %pad_maximum_fusion.factor = f32[48,128,128]{2,1,0:T(8,128)S(1)} fusion(f32[48,128,64]{2,1,0:T(8,128)} %get-tuple-element.79, f32[48,128,64]{2,1,0:T(8,128)} %get-tuple-element.78), kind=kLoop, calls=%fused_computation.4 | loop fusion | flops 786432 | bytes 6291456 | tf_op jit(solution)/shard_map/concatenate | solution.py:378
  54.6 0.9 copy-done.4
  55.5 2.8 shard_map.104
  59.0 14.7 %all-to-all-start.1 = ((f32[256,1,128]{2,1,0:T(1,128)}), f32[256,1,128]{2,1,0:T(1,128)}, u32[]{:S(2)}, u32[]{:S(2)}) async-start(f32[256,1,128]{2,1,0:T(1,128)} %bitcast.113), calls=%async_computation.1 | async-start | bytes 262144 | tf_op jit(solution)/shard_map/all_to_all | solution.py:336
  74.3 1.3 slice_bitcast_fusion.1.refs_17_
  77.1 5.8 %all-to-all-done.1 = f32[256,1,128]{2,1,0:T(1,128)} async-done(((f32[256,1,128]{2,1,0:T(1,128)}), f32[256,1,128]{2,1,0:T(1,128)}, u32[]{:S(2)}, u32[]{:S(2)}) %all-to-all-start.1) | async-done | bytes 131104 | tf_op jit(solution)/shard_map/all_to_all | solution.py:336
  83.6 3.4 %copy-done = bf16[4,4,512,512]{3,2,1,0:T(8,128)(2,1)S(1)} copy-done((bf16[4,4,512,512]{3,2,1,0:T(8,128)(2,1)S(1)}, bf16[4,4,512,512]{3,2,1,0:T(8,128)(2,1)}, u32[]{:S(2)}) %copy-start) | copy-done | bytes 8388632
  93.3 2.5 shard_map.105
  95.9 18.2 %all_to_all.85 = f32[256,1,128]{2,1,0:T(1,128)S(1)} all-to-all(f32[256,1,128]{2,1,0:T(1,128)S(1)} %bitcast.116), channel_id=1, replica_groups=mesh['gx'=32,'gy'=8] {'gx','gy'}, dimensions={0} | all-to-all | bytes 262144 | tf_op jit(solution)/shard_map/all_to_all | solution.py:336
  114.1 1.6 shard_map.106
  116.4 10.1 %all-to-all-start.3 = ((f32[256,1,128]{2,1,0:T(1,128)}), f32[256,1,128]{2,1,0:T(1,128)}, u32[]{:S(2)}, u32[]{:S(2)}) async-start(f32[256,1,128]{2,1,0:T(1,128)} %bitcast.111), calls=%async_computation.3 | async-start | bytes 262144 | tf_op jit(solution)/shard_map/all_to_all | solution.py:336
  127.2 6.7 %collective-permute-start.4 = (f32[16,128]{1,0:T(8,128)S(1)}, f32[16,128]{1,0:T(8,128)S(1)}, u32[]{:S(2)}, u32[]{:S(2)}) collective-permute-start(f32[16,128]{1,0:T(8,128)S(1)} %get-tuple-element.93), channel_id=1, source_target_pairs={{8,0},{16,8},{24,16},{32,24},{40,32},{48,40},{56,48},{64,56},{72,6... | collective-permute-start | bytes 24584 | tf_op jit(solution)/shard_map/ppermute | solution.py:341
  134.6 1.9 collective-permute-start.5
  136.5 2.2 collective-permute-start.6
  138.8 2.1 collective-permute-start.7
  144.3 3.4 %copy-done.1 = bf16[4,4,512,512]{3,2,1,0:T(8,128)(2,1)S(1)} copy-done((bf16[4,4,512,512]{3,2,1,0:T(8,128)(2,1)S(1)}, bf16[4,4,512,512]{3,2,1,0:T(8,128)(2,1)}, u32[]{:S(2)}) %copy-start.1) | copy-done | bytes 8388632
  156.9 2.5 shard_map.107
  159.5 20.6 %all_to_all.86 = f32[256,1,128]{2,1,0:T(1,128)S(1)} all-to-all(f32[256,1,128]{2,1,0:T(1,128)S(1)} %bitcast.115), channel_id=1, replica_groups=mesh['gx'=32,'gy'=8] {'gx','gy'}, dimensions={0} | all-to-all | bytes 262144 | tf_op jit(solution)/shard_map/all_to_all | solution.py:336
  180.1 1.2 shard_map.108
  182.4 10.1 %all-to-all-start.5 = ((f32[256,1,128]{2,1,0:T(1,128)}), f32[256,1,128]{2,1,0:T(1,128)}, u32[]{:S(2)}, u32[]{:S(2)}) async-start(f32[256,1,128]{2,1,0:T(1,128)} %bitcast.112), calls=%async_computation.5 | async-start | bytes 262144 | tf_op jit(solution)/shard_map/all_to_all | solution.py:336
  193.2 2.5 collective-permute-start.10
  196.5 1.9 collective-permute-start.11
  198.4 6.7 %collective-permute-start.8 = (f32[16,128]{1,0:T(8,128)S(1)}, f32[16,128]{1,0:T(8,128)S(1)}, u32[]{:S(2)}, u32[]{:S(2)}) collective-permute-start(f32[16,128]{1,0:T(8,128)S(1)} %get-tuple-element.91), channel_id=1, source_target_pairs={{8,0},{16,8},{24,16},{32,24},{40,32},{48,40},{56,48},{64,56},{72,6... | collective-permute-start | bytes 24584 | tf_op jit(solution)/shard_map/ppermute | solution.py:341
  205.1 1.9 collective-permute-start.9
  208.8 3.9 %collective-permute-done.9.refs_22_ = f32[16,128]{1,0:T(8,128)S(1)} collective-permute-done((f32[16,128]{1,0:T(8,128)S(1)}, f32[16,128]{1,0:T(8,128)S(1)}, u32[]{:S(2)}, u32[]{:S(2)}) %collective-permute-start.9) | collective-permute-done | bytes 8224 | tf_op jit(solution)/shard_map/ppermute | solution.py:346
  213.3 3.4 %copy-done.2 = bf16[4,4,512,512]{3,2,1,0:T(8,128)(2,1)S(1)} copy-done((bf16[4,4,512,512]{3,2,1,0:T(8,128)(2,1)S(1)}, bf16[4,4,512,512]{3,2,1,0:T(8,128)(2,1)}, u32[]{:S(2)}) %copy-start.2) | copy-done | bytes 8388632
  228.0 2.9 shard_map.109
  230.9 18.0 %all_to_all.87 = f32[256,1,128]{2,1,0:T(1,128)S(1)} all-to-all(f32[256,1,128]{2,1,0:T(1,128)S(1)} %bitcast.114), channel_id=1, replica_groups=mesh['gx'=32,'gy'=8] {'gx','gy'}, dimensions={0} | all-to-all | bytes 262144 | tf_op jit(solution)/shard_map/all_to_all | solution.py:336
  248.9 1.2 shard_map.110
  251.2 8.5 %all-to-all-start.7 = ((f32[256,1,128]{2,1,0:T(1,128)}), f32[256,1,128]{2,1,0:T(1,128)S(1)}, u32[]{:S(2)}, u32[]{:S(2)}) async-start(f32[256,1,128]{2,1,0:T(1,128)} %bitcast.110), calls=%async_computation.7 | async-start | bytes 262144 | tf_op jit(solution)/shard_map/all_to_all | solution.py:336
  260.5 6.7 %collective-permute-start.12 = (f32[16,128]{1,0:T(8,128)S(1)}, f32[16,128]{1,0:T(8,128)S(1)}, u32[]{:S(2)}, u32[]{:S(2)}) collective-permute-start(f32[16,128]{1,0:T(8,128)S(1)} %get-tuple-element.89), channel_id=1, source_target_pairs={{8,0},{16,8},{24,16},{32,24},{40,32},{48,40},{56,48},{64,56},{72,6... | collective-permute-start | bytes 24584 | tf_op jit(solution)/shard_map/ppermute | solution.py:341
  267.9 1.9 collective-permute-start.13
  269.8 2.2 collective-permute-start.14
  272.0 2.1 collective-permute-start.15
  274.2 1.4 collective-permute-done.13.refs_25_
  275.5 1.5 collective-permute-done.15.refs_27_
  288.1 1.2 shard_map.111
  (228 shorter events, 64.4 us)
Async XLA Ops:
  5.7 71.3 %collective-permute-start = (f32[3,16,128]{2,1,0:T(8,128)}, f32[3,16,128]{2,1,0:T(8,128)}, u32[]{:S(2)}, u32[]{:S(2)}) collective-permute-start(f32[3,16,128]{2,1,0:T(8,128)} %get-tuple-element.38.refs_7_), channel_id=1, source_target_pairs={{8,0},{16,8},{24,16},{32,24},{40,32},{48,40},{56,48},{64,56},{72,6... | collective-permute-start | bytes 73736 | tf_op jit(solution)/shard_map/ppermute | solution.py:341
  13.7 63.4 %collective-permute-start.2 = (f32[3,16,128]{2,1,0:T(8,128)}, f32[3,16,128]{2,1,0:T(8,128)}, u32[]{:S(2)}, u32[]{:S(2)}) collective-permute-start(f32[3,16,128]{2,1,0:T(8,128)} %get-tuple-element.39.refs_8_), channel_id=1, source_target_pairs={{1,0},{2,1},{3,2},{4,3},{5,4},{6,5},{7,6},{9,8},{10,9},{11,10},{12... | collective-permute-start | bytes 73736 | tf_op jit(solution)/shard_map/ppermute | solution.py:341
  17.6 56.7 %collective-permute-start.1 = (f32[4,16,128]{2,1,0:T(8,128)}, f32[4,16,128]{2,1,0:T(8,128)}, u32[]{:S(2)}, u32[]{:S(2)}) collective-permute-start(f32[4,16,128]{2,1,0:T(8,128)} %pad_maximum_fusion.1), channel_id=1, source_target_pairs={{0,8},{8,16},{16,24},{24,32},{32,40},{40,48},{48,56},{56,64},{64,7... | collective-permute-start | bytes 98312 | tf_op jit(solution)/shard_map/ppermute | solution.py:346
  20.1 53.6 %collective-permute-start.3 = (f32[4,16,128]{2,1,0:T(8,128)}, f32[4,16,128]{2,1,0:T(8,128)S(1)}, u32[]{:S(2)}, u32[]{:S(2)}) collective-permute-start(f32[4,16,128]{2,1,0:T(8,128)} %pad_maximum_fusion.2), channel_id=1, source_target_pairs={{0,1},{1,2},{2,3},{3,4},{4,5},{5,6},{6,7},{8,9},{9,10},{10,11},{11... | collective-permute-start | bytes 98312 | tf_op jit(solution)/shard_map/ppermute | solution.py:346
  25.5 28.5 %all-to-all-start = ((f32[256,1,128]{2,1,0:T(1,128)}), f32[256,1,128]{2,1,0:T(1,128)S(1)}, u32[]{:S(2)}, u32[]{:S(2)}) async-start(f32[256,1,128]{2,1,0:T(1,128)} %broadcast_in_dim.28), calls=%async_computation | async-start | bytes 262144 | tf_op jit(solution)/shard_map/all_to_all | solution.py:336
  54.6 0.9 copy-start.4
  59.0 23.9 %all-to-all-start.1 = ((f32[256,1,128]{2,1,0:T(1,128)}), f32[256,1,128]{2,1,0:T(1,128)}, u32[]{:S(2)}, u32[]{:S(2)}) async-start(f32[256,1,128]{2,1,0:T(1,128)} %bitcast.113), calls=%async_computation.1 | async-start | bytes 262144 | tf_op jit(solution)/shard_map/all_to_all | solution.py:336
  83.6 12.2 %copy-start.17 = (f32[16,128]{1,0:T(8,128)}, f32[16,128]{1,0:T(8,128)S(1)}, u32[]{:S(2)}) copy-start(f32[16,128]{1,0:T(8,128)S(1)} %iota.15.refs_0_) | copy-start | bytes 24580
  83.6 3.4 %copy-start = (bf16[4,4,512,512]{3,2,1,0:T(8,128)(2,1)S(1)}, bf16[4,4,512,512]{3,2,1,0:T(8,128)(2,1)}, u32[]{:S(2)}) copy-start(bf16[4,4,512,512]{3,2,1,0:T(8,128)(2,1)} %param.8) | copy-start | bytes 25165828
  95.8 19.9 %copy-start.40 = (f32[4,16,128]{2,1,0:T(8,128)}, f32[4,16,128]{2,1,0:T(8,128)S(1)}, u32[]{:S(2)}) copy-start(f32[4,16,128]{2,1,0:T(8,128)S(1)} %get-tuple-element.46.refs_16_) | copy-start | bytes 98308
  95.9 20.5 %copy-start.46 = (f32[2,16,128]{2,1,0:T(8,128)}, f32[2,16,128]{2,1,0:T(8,128)S(1)}, u32[]{:S(2)}) copy-start(f32[2,16,128]{2,1,0:T(8,128)S(1)} %get-tuple-element.47.refs_17_) | copy-start | bytes 49156
  95.9 20.5 %copy-start.50 = (f32[4,16,128]{2,1,0:T(8,128)}, f32[4,16,128]{2,1,0:T(8,128)S(1)}, u32[]{:S(2)}) copy-start(f32[4,16,128]{2,1,0:T(8,128)S(1)} %get-tuple-element.45.refs_15_) | copy-start | bytes 98308
  95.9 20.5 %copy-start.56 = (f32[2,16,128]{2,1,0:T(8,128)}, f32[2,16,128]{2,1,0:T(8,128)S(1)}, u32[]{:S(2)}) copy-start(f32[2,16,128]{2,1,0:T(8,128)S(1)} %get-tuple-element.51.refs_16_) | copy-start | bytes 49156
  116.4 27.9 %all-to-all-start.3 = ((f32[256,1,128]{2,1,0:T(1,128)}), f32[256,1,128]{2,1,0:T(1,128)}, u32[]{:S(2)}, u32[]{:S(2)}) async-start(f32[256,1,128]{2,1,0:T(1,128)} %bitcast.111), calls=%async_computation.3 | async-start | bytes 262144 | tf_op jit(solution)/shard_map/all_to_all | solution.py:336
  127.2 13.7 %collective-permute-start.4 = (f32[16,128]{1,0:T(8,128)S(1)}, f32[16,128]{1,0:T(8,128)S(1)}, u32[]{:S(2)}, u32[]{:S(2)}) collective-permute-start(f32[16,128]{1,0:T(8,128)S(1)} %get-tuple-element.93), channel_id=1, source_target_pairs={{8,0},{16,8},{24,16},{32,24},{40,32},{48,40},{56,48},{64,56},{72,6... | collective-permute-start | bytes 24584 | tf_op jit(solution)/shard_map/ppermute | solution.py:341
  134.6 7.6 %collective-permute-start.5 = (f32[16,128]{1,0:T(8,128)S(1)}, f32[16,128]{1,0:T(8,128)S(1)}, u32[]{:S(2)}, u32[]{:S(2)}) collective-permute-start(f32[16,128]{1,0:T(8,128)S(1)} %get-tuple-element.87), channel_id=1, source_target_pairs={{0,8},{8,16},{16,24},{24,32},{32,40},{40,48},{48,56},{56,64},{64,7... | collective-permute-start | bytes 24584 | tf_op jit(solution)/shard_map/ppermute | solution.py:346
  136.5 6.3 %collective-permute-start.6 = (f32[16,128]{1,0:T(8,128)S(1)}, f32[16,128]{1,0:T(8,128)S(1)}, u32[]{:S(2)}, u32[]{:S(2)}) collective-permute-start(f32[16,128]{1,0:T(8,128)S(1)} %get-tuple-element.92), channel_id=1, source_target_pairs={{1,0},{2,1},{3,2},{4,3},{5,4},{6,5},{7,6},{9,8},{10,9},{11,10},{12... | collective-permute-start | bytes 24584 | tf_op jit(solution)/shard_map/ppermute | solution.py:341
  138.8 5.0 %collective-permute-start.7 = (f32[16,128]{1,0:T(8,128)S(1)}, f32[16,128]{1,0:T(8,128)S(1)}, u32[]{:S(2)}, u32[]{:S(2)}) collective-permute-start(f32[16,128]{1,0:T(8,128)S(1)} %get-tuple-element.86), channel_id=1, source_target_pairs={{0,1},{1,2},{2,3},{3,4},{4,5},{5,6},{6,7},{8,9},{9,10},{10,11},{11... | collective-permute-start | bytes 24584 | tf_op jit(solution)/shard_map/ppermute | solution.py:346
  144.3 3.4 %copy-start.1 = (bf16[4,4,512,512]{3,2,1,0:T(8,128)(2,1)S(1)}, bf16[4,4,512,512]{3,2,1,0:T(8,128)(2,1)}, u32[]{:S(2)}) copy-start(bf16[4,4,512,512]{3,2,1,0:T(8,128)(2,1)} %param.8) | copy-start | bytes 25165828
  151.9 0.8 copy-start.41
  153.4 0.8 copy-start.51
  159.4 21.8 %copy-start.21 = (f32[4,16,128]{2,1,0:T(8,128)}, f32[4,16,128]{2,1,0:T(8,128)S(1)}, u32[]{:S(2)}) copy-start(f32[4,16,128]{2,1,0:T(8,128)S(1)} %get-tuple-element.53.refs_18_.refs_19_) | copy-start | bytes 98308
  159.4 22.5 %copy-start.38 = (f32[4,16,128]{2,1,0:T(8,128)}, f32[4,16,128]{2,1,0:T(8,128)S(1)}, u32[]{:S(2)}) copy-start(f32[4,16,128]{2,1,0:T(8,128)S(1)} %get-tuple-element.54.refs_19_) | copy-start | bytes 98308
  159.5 22.5 %copy-start.44 = (f32[2,16,128]{2,1,0:T(8,128)}, f32[2,16,128]{2,1,0:T(8,128)S(1)}, u32[]{:S(2)}) copy-start(f32[2,16,128]{2,1,0:T(8,128)S(1)} %get-tuple-element.55.refs_20_) | copy-start | bytes 49156
  159.5 22.5 %copy-start.87 = (f32[1,128]{1,0:T(1,128)}, f32[1,128]{1,0:T(1,128)S(1)}, u32[]{:S(2)}) copy-start(f32[1,128]{1,0:T(1,128)S(1)} %get-tuple-element.52.refs_17_) | copy-start | bytes 1540
  182.4 30.9 %all-to-all-start.5 = ((f32[256,1,128]{2,1,0:T(1,128)}), f32[256,1,128]{2,1,0:T(1,128)}, u32[]{:S(2)}, u32[]{:S(2)}) async-start(f32[256,1,128]{2,1,0:T(1,128)} %bitcast.112), calls=%async_computation.5 | async-start | bytes 262144 | tf_op jit(solution)/shard_map/all_to_all | solution.py:336
  193.2 13.8 %collective-permute-start.10 = (f32[16,128]{1,0:T(8,128)S(1)}, f32[16,128]{1,0:T(8,128)S(1)}, u32[]{:S(2)}, u32[]{:S(2)}) collective-permute-start(f32[16,128]{1,0:T(8,128)S(1)} %get-tuple-element.90), channel_id=1, source_target_pairs={{1,0},{2,1},{3,2},{4,3},{5,4},{6,5},{7,6},{9,8},{10,9},{11,10},{12... | collective-permute-start | bytes 24584 | tf_op jit(solution)/shard_map/ppermute | solution.py:341
  196.5 11.2 %collective-permute-start.11 = (f32[16,128]{1,0:T(8,128)S(1)}, f32[16,128]{1,0:T(8,128)S(1)}, u32[]{:S(2)}, u32[]{:S(2)}) collective-permute-start(f32[16,128]{1,0:T(8,128)S(1)} %get-tuple-element.84), channel_id=1, source_target_pairs={{0,1},{1,2},{2,3},{3,4},{4,5},{5,6},{6,7},{8,9},{9,10},{10,11},{11... | collective-permute-start | bytes 24584 | tf_op jit(solution)/shard_map/ppermute | solution.py:346
  198.4 9.8 %collective-permute-start.8 = (f32[16,128]{1,0:T(8,128)S(1)}, f32[16,128]{1,0:T(8,128)S(1)}, u32[]{:S(2)}, u32[]{:S(2)}) collective-permute-start(f32[16,128]{1,0:T(8,128)S(1)} %get-tuple-element.91), channel_id=1, source_target_pairs={{8,0},{16,8},{24,16},{32,24},{40,32},{48,40},{56,48},{64,56},{72,6... | collective-permute-start | bytes 24584 | tf_op jit(solution)/shard_map/ppermute | solution.py:341
  205.1 7.7 %collective-permute-start.9 = (f32[16,128]{1,0:T(8,128)S(1)}, f32[16,128]{1,0:T(8,128)S(1)}, u32[]{:S(2)}, u32[]{:S(2)}) collective-permute-start(f32[16,128]{1,0:T(8,128)S(1)} %get-tuple-element.85), channel_id=1, source_target_pairs={{0,8},{8,16},{16,24},{24,32},{32,40},{40,48},{48,56},{56,64},{64,7... | collective-permute-start | bytes 24584 | tf_op jit(solution)/shard_map/ppermute | solution.py:346
  213.3 3.4 %copy-start.2 = (bf16[4,4,512,512]{3,2,1,0:T(8,128)(2,1)S(1)}, bf16[4,4,512,512]{3,2,1,0:T(8,128)(2,1)}, u32[]{:S(2)}) copy-start(bf16[4,4,512,512]{3,2,1,0:T(8,128)(2,1)} %param.8) | copy-start | bytes 25165828
  219.5 0.8 copy-start.22
  221.7 0.8 copy-start.39
  230.8 19.2 %copy-start.42 = (f32[4,16,128]{2,1,0:T(8,128)}, f32[4,16,128]{2,1,0:T(8,128)S(1)}, u32[]{:S(2)}) copy-start(f32[4,16,128]{2,1,0:T(8,128)S(1)} %get-tuple-element.64.refs_22_) | copy-start | bytes 98308
  230.8 19.9 %copy-start.48 = (f32[2,16,128]{2,1,0:T(8,128)}, f32[2,16,128]{2,1,0:T(8,128)S(1)}, u32[]{:S(2)}) copy-start(f32[2,16,128]{2,1,0:T(8,128)S(1)} %get-tuple-element.65.refs_23_) | copy-start | bytes 49156
  230.8 19.9 %copy-start.58 = (f32[2,16,128]{2,1,0:T(8,128)}, f32[2,16,128]{2,1,0:T(8,128)S(1)}, u32[]{:S(2)}) copy-start(f32[2,16,128]{2,1,0:T(8,128)S(1)} %get-tuple-element.59.refs_16_) | copy-start | bytes 49156
  230.9 19.9 %copy-start.60 = (f32[2,16,128]{2,1,0:T(8,128)}, f32[2,16,128]{2,1,0:T(8,128)S(1)}, u32[]{:S(2)}) copy-start(f32[2,16,128]{2,1,0:T(8,128)S(1)} %get-tuple-element.62.refs_20_) | copy-start | bytes 49156
  230.9 19.9 %copy-start.62 = (f32[2,16,128]{2,1,0:T(8,128)}, f32[2,16,128]{2,1,0:T(8,128)S(1)}, u32[]{:S(2)}) copy-start(f32[2,16,128]{2,1,0:T(8,128)S(1)} %get-tuple-element.63.refs_21_) | copy-start | bytes 49156
  230.9 19.9 %copy-start.83 = (f32[1,128]{1,0:T(1,128)}, f32[1,128]{1,0:T(1,128)S(1)}, u32[]{:S(2)}) copy-start(f32[1,128]{1,0:T(1,128)S(1)} %get-tuple-element.60.refs_17_) | copy-start | bytes 1540
  230.9 19.9 %copy-start.85 = (f32[1,128]{1,0:T(1,128)}, f32[1,128]{1,0:T(1,128)S(1)}, u32[]{:S(2)}) copy-start(f32[1,128]{1,0:T(1,128)S(1)} %get-tuple-element.61.refs_18_) | copy-start | bytes 1540
  251.2 25.8 %all-to-all-start.7 = ((f32[256,1,128]{2,1,0:T(1,128)}), f32[256,1,128]{2,1,0:T(1,128)S(1)}, u32[]{:S(2)}, u32[]{:S(2)}) async-start(f32[256,1,128]{2,1,0:T(1,128)} %bitcast.110), calls=%async_computation.7 | async-start | bytes 262144 | tf_op jit(solution)/shard_map/all_to_all | solution.py:336
  260.5 13.7 %collective-permute-start.12 = (f32[16,128]{1,0:T(8,128)S(1)}, f32[16,128]{1,0:T(8,128)S(1)}, u32[]{:S(2)}, u32[]{:S(2)}) collective-permute-start(f32[16,128]{1,0:T(8,128)S(1)} %get-tuple-element.89), channel_id=1, source_target_pairs={{8,0},{16,8},{24,16},{32,24},{40,32},{48,40},{56,48},{64,56},{72,6... | collective-permute-start | bytes 24584 | tf_op jit(solution)/shard_map/ppermute | solution.py:341
  267.9 7.6 %collective-permute-start.13 = (f32[16,128]{1,0:T(8,128)S(1)}, f32[16,128]{1,0:T(8,128)S(1)}, u32[]{:S(2)}, u32[]{:S(2)}) collective-permute-start(f32[16,128]{1,0:T(8,128)S(1)} %get-tuple-element.83), channel_id=1, source_target_pairs={{0,8},{8,16},{16,24},{24,32},{32,40},{40,48},{48,56},{56,64},{64,7... | collective-permute-start | bytes 24584 | tf_op jit(solution)/shard_map/ppermute | solution.py:346
  269.8 5.7 %collective-permute-start.14 = (f32[16,128]{1,0:T(8,128)S(1)}, f32[16,128]{1,0:T(8,128)S(1)}, u32[]{:S(2)}, u32[]{:S(2)}) collective-permute-start(f32[16,128]{1,0:T(8,128)S(1)} %get-tuple-element.88), channel_id=1, source_target_pairs={{1,0},{2,1},{3,2},{4,3},{5,4},{6,5},{7,6},{9,8},{10,9},{11,10},{12... | collective-permute-start | bytes 24584 | tf_op jit(solution)/shard_map/ppermute | solution.py:341
  272.0 5.0 %collective-permute-start.15 = (f32[16,128]{1,0:T(8,128)S(1)}, f32[16,128]{1,0:T(8,128)S(1)}, u32[]{:S(2)}, u32[]{:S(2)}) collective-permute-start(f32[16,128]{1,0:T(8,128)S(1)} %get-tuple-element.82), channel_id=1, source_target_pairs={{0,1},{1,2},{2,3},{3,4},{4,5},{5,6},{6,7},{8,9},{9,10},{10,11},{11... | collective-permute-start | bytes 24584 | tf_op jit(solution)/shard_map/ppermute | solution.py:346
  279.8 0.8 copy-start.23
  282.0 0.8 copy-start.43
  282.7 0.7 copy-start.49
  (65 other events, 43.4 us)
where the time goes:
time: 296 us; the launch traced here: 291 us
  starting transfers between devices  108 us (36%)
  local copies, waits for them, and re-layouts  87.6 us (30%)
  blocking collectives  56.7 us (19%)
  Pallas kernels  17.3 us (6%)
  waiting for transfers between devices  13.7 us (5%)
  other arithmetic  6.88 us (2%)
    unnamed x190, local copies, waits for them, and re-layouts  63.4 us
    all_to_all x3, blocking collectives, exchange(): return lax.all_to_all(rows, ALL, split_axis=0, concat_axis=0, tiled=True)  56.7 us
    all_to_all x5, starting transfers between devices, exchange(): return lax.all_to_all(rows, ALL, split_axis=0, concat_axis=0, tiled=True)  54.4 us
    ppermute x8, starting transfers between devices, from_next(): return lax.ppermute(value, axis, [(i + 1, i) for i in range(n - 1)])  36.8 us
    pallas_call x9, Pallas kernels, call(): pl.pallas_call(kernel, out_shape=outs, in_specs=[pl.BlockSpec(memory_spac...  17.3 us
    ppermute x8, starting transfers between devices, from_previous(): return lax.ppermute(value, axis, [(i, i + 1) for i in range(n - 1)])  16.7 us
    ppermute x8, waiting for transfers between devices, from_previous(): return lax.ppermute(value, axis, [(i, i + 1) for i in range(n - 1)])  7.84 us
    squeeze x1, local copies, waits for them, and re-layouts, shards(): factor = jnp.concatenate([blocks[:, 0], blocks[:, 1]], axis=-1)  6.63 us
  transfers between devices with their start and end apart: 21, of which 6 were waited for; matrix products, arithmetic and copies ran while one was open for 10% of the time, Pallas kernels for 1%

commit v1 on v0

v1 whole, which is shorter than its diff:
```python
import jax
import jax.numpy as jnp
from jax import lax
from jax.experimental import pallas as pl
from jax.experimental.pallas import tpu as pltpu
from jax.sharding import PartitionSpec as P

GX, GY = "gx", "gy"
ALL = (GX, GY)
SUB = 16
E = 128
MODES = 3
BLOCK = 48
PEERS = 256
LANES = 128

AT_W, AT_E, AT_S, AT_N, AT_EDGE, AT_SCALAR = 48, 60, 72, 84, 96, 104
EDGES_SETUP = (3, 4, 3, 4)
EDGES = (1, 1, 1, 1)


def lane_gather(values, index):
    return jnp.take_along_axis(values, index, axis=1)


def up(values, rows):
    return pltpu.roll(values, values.shape[0] - rows, 0)


def down(values, rows):
    return pltpu.roll(values, rows, 0)


KEEP_W, KEEP_S, M, TMW, TMS, NB_TMW, NB_ME, NB_TMS, NB_MN, TARGET = 0, 1, 2, 14, 17, 20, 23, 26, 29, 32
PACKED = 36
WMAP, SMAP, WINV, SINV = range(4)


class Local:
    def __init__(self, maps, pack):
        self.maps, self.pack = maps, pack
        s = lax.broadcasted_iota(jnp.int32, (SUB, LANES), 0)
        self.lane = lax.broadcasted_iota(jnp.int32, (SUB, LANES), 1)
        self.s, self.x, self.y = s, lax.shift_right_logical(s, 2), lax.bitwise_and(s, 3)

    def own_at(self, r):
        return 3 * self.s + r

    def west_at(self, r):
        return AT_W + 3 * self.y + r

    def east_at(self, r):
        return AT_E + 3 * self.y + r

    def south_at(self, r):
        return AT_S + 3 * self.x + r

    def north_at(self, r):
        return AT_N + 3 * self.x + r

    def cross(self, w, t, nb):
        x, y = self.x, self.y
        nb_tw, nb_we, nb_ts, nb_wn = nb
        east = w[1] - up(jnp.where(x == 0, nb_tw, t[0]), 4)
        north = w[3] - jnp.where(y == 3, down(nb_ts, 3), up(t[1], 1))
        from_west = down(jnp.where(x == 3, nb_we, w[1]), 4)
        from_south = jnp.where(y == 0, up(nb_wn, 3), down(w[3], 1))
        west = self.pack[KEEP_W] * (w[0] - lane_gather(from_west, self.maps[WMAP]))
        south = self.pack[KEEP_S] * (w[2] - lane_gather(from_south, self.maps[SMAP]))
        return west, east, south, north

    def modes(self, r, side):
        return self.pack[M + 4 * r + side]

    def lift(self, row):
        a = jnp.broadcast_to(row, (SUB, LANES))
        pack = self.pack
        w = [0.0] * 4
        t = [0.0] * 2
        nb = [0.0] * 4
        for r in range(MODES):
            own = lane_gather(a, self.own_at(r))
            for side in range(4):
                w[side] += self.modes(r, side) * own
            t[0] += pack[TMW + r] * own
            t[1] += pack[TMS + r] * own
            nb[0] += pack[NB_TMW + r] * lane_gather(a, self.east_at(r))
            nb[1] += pack[NB_ME + r] * lane_gather(a, self.west_at(r))
            nb[2] += pack[NB_TMS + r] * lane_gather(a, self.north_at(r))
            nb[3] += pack[NB_MN + r] * lane_gather(a, self.south_at(r))
        return self.cross(w, t, nb)

    def put(self, total, values, at, rows=None):
        here = self.lane == at
        if rows is not None:
            here = here & rows
        return total + jnp.where(here, jnp.sum(values, axis=1, keepdims=True), 0.0)

    def absorb(self, total, u):
        for r in range(MODES):
            terms = sum(self.modes(r, side) * u[side] for side in range(4))
            total = self.put(total, terms, self.own_at(r))
        return total

    def contributions(self, w, t):
        pack, x, y = self.pack, self.x, self.y
        none = jnp.zeros((SUB, LANES), jnp.float32)
        total = self.absorb(none, self.cross(w, t, (none, none, none, none)))
        to_e, to_w = down(w[1], 4), up(t[0], 4)
        to_n, to_s = up(w[3], 3), down(t[1], 3)
        for r in range(MODES):
            total = self.put(total, -pack[NB_TMW + r] * to_e, self.east_at(r), x == 0)
            total = self.put(total, -pack[NB_ME + r] * to_w, self.west_at(r), x == 3)
            total = self.put(total, -pack[NB_TMS + r] * to_n, self.north_at(r), y == 0)
            total = self.put(total, -pack[NB_MN + r] * to_s, self.south_at(r), y == 3)
        return total

    def dual(self, u, operators, precise):
        whole = jnp.concatenate(u, axis=1)
        left = whole.astype(jnp.bfloat16)
        if precise:
            rest = (whole - left.astype(jnp.float32)).astype(jnp.bfloat16)
            left = jnp.concatenate([left, rest], axis=0)
        row = lax.broadcasted_iota(jnp.int32, (SUB, 4 * E), 0)
        out = jnp.zeros((SUB, 4 * E), jnp.float32)
        for k in range(SUB):
            product = jnp.dot(left, operators.get(k), preferred_element_type=jnp.float32)
            if precise:
                product = product[:SUB] + product[SUB:]
            out = jnp.where(row == k, product, out)
        w = [out[:, side * E : (side + 1) * E] for side in range(4)]
        t = lane_gather(w[0], self.maps[WINV]), lane_gather(w[2], self.maps[SINV])
        return w, t

    def send(self, total, edges, ref):
        send_rows(jnp.sum(total, axis=0, keepdims=True), edges, ref)


class Operators:
    def __init__(self, source, held, arrived):
        self.held = held
        self.copies = []
        for k in range(SUB):
            copy = pltpu.make_async_copy(source.at[k // 4, k % 4], held.at[k], arrived.at[k])
            copy.start()
            self.copies.append(copy)

    def get(self, k):
        self.copies[k].wait()
        return self.held[k]


EDGE_ROWS = ([0, 1, 2, 3], [12, 13, 14, 15], [0, 4, 8, 12], [3, 7, 11, 15])


def send_rows(row, edges, ref):
    at_x, at_y = lax.axis_index(GX), lax.axis_index(GY)
    no_one = (at_x == 0, at_x == lax.axis_size(GX) - 1, at_y == 0, at_y == lax.axis_size(GY) - 1)
    for half in range(2):
        parts = []
        for arrays, rows, none in zip(edges, EDGE_ROWS, no_one):
            for array in arrays:
                for k in (half, half + 2):
                    parts.append(jnp.where(none, 0.0, array[rows[k] : rows[k] + 1]))
        count = len(parts)
        before, rest = jnp.zeros((AT_EDGE, LANES), jnp.float32), LANES - AT_EDGE - count
        parts = [before, *parts, jnp.zeros((rest, LANES), jnp.float32)]
        turned = jnp.concatenate(parts, axis=0).T
        lane = lax.broadcasted_iota(jnp.int32, (LANES, LANES), 1)
        here = (lane >= AT_EDGE) & (lane < AT_EDGE + count)
        ref[half * LANES : (half + 1) * LANES, :] = jnp.where(here, turned, row)


def arrived_edges(ref, counts):
    halves = [ref[half * LANES : (half + 1) * LANES, :].T for half in range(2)]
    s = lax.broadcasted_iota(jnp.int32, (SUB, LANES), 0)
    at = AT_EDGE
    out = []
    for count, place in zip(counts, (lax.bitwise_and(s, 3),) * 2 + (lax.shift_right_logical(s, 2),) * 2):
        arrays = []
        for _ in range(count):
            rows = [halves[k % 2][at + k // 2 : at + k // 2 + 1] for k in range(4)]
            arrays.append(
                jnp.where(place == 0, rows[0], jnp.where(place == 1, rows[1], jnp.where(place == 2, rows[2], rows[3])))
            )
            at += 2
        out.append(arrays)
    return out


def pass_on(entries, lane, counts):
    ends = []
    at = AT_EDGE
    for count in counts:
        at += 2 * count
        ends.append(at)
    moved = jnp.where(lane < ends[2], up(entries, 1), down(entries, 1))
    return jnp.where(lane < ends[0], up(entries, 8), jnp.where(lane < ends[1], down(entries, 8), moved))


def from_peers(ref):
    return jnp.sum(ref[...], axis=0, keepdims=True)


def scalar(ref, i):
    return ref[0:1, AT_SCALAR + i : AT_SCALAR + i + 1]


def keep(ref, *parts):
    for i, part in enumerate(parts):
        ref[i] = jnp.broadcast_to(part, (SUB, LANES))


LOAD_E, LOAD_N, KEPT = 20, 21, 22


def start_kernel(loads, owner, west_map, south_map, images, load, out, maps, kept):
    lane = lax.broadcasted_iota(jnp.int32, (E, E), 1)
    at = lax.broadcasted_iota(jnp.int32, (E, E), 0)
    for source, direct, inverse in ((west_map, WMAP, WINV), (south_map, SMAP, SINV)):
        rows = jnp.concatenate([source[x] for x in range(4)], axis=0)
        maps[direct] = rows
        columns = jnp.concatenate([rows, jnp.zeros((E - SUB, E), jnp.int32)], axis=0).T
        found = []
        for k in range(SUB):
            hit = columns[:, k : k + 1] == lane
            found.append(jnp.sum(jnp.where(hit, at, 0), axis=0, keepdims=True))
        maps[inverse] = jnp.concatenate(found, axis=0)
    s = lax.broadcasted_iota(jnp.int32, (SUB, LANES), 0)
    first_x, first_y = lax.axis_index(GX) == 0, lax.axis_index(GY) == 0
    kept[KEEP_W] = jnp.where(first_x & (s < 4), 0.0, 1.0)
    kept[KEEP_S] = jnp.where(first_y & (lax.bitwise_and(s, 3) == 0), 0.0, 1.0)
    for r in range(MODES):
        whole = jnp.concatenate([images[x, r] for x in range(4)], axis=0)
        for side in range(4):
            kept[M + 4 * r + side] = whole[:, side * E : (side + 1) * E]
        kept[TMW + r] = lane_gather(whole[:, :E], maps[WINV])
        kept[TMS + r] = lane_gather(whole[:, 2 * E : 3 * E], maps[SINV])
    kept[LOAD_E] = jnp.concatenate([load[k // 4, k % 4, 0:1, :] for k in range(SUB)], axis=0)
    kept[LOAD_N] = jnp.concatenate([load[k // 4, k % 4, 1:2, :] for k in range(SUB)], axis=0)

    x = lax.broadcasted_iota(jnp.int32, (8, LANES), 0)
    lane8 = lax.broadcasted_iota(jnp.int32, (8, LANES), 1)
    off = lane8 - 12 * x
    y = sum((off >= c).astype(jnp.int32) for c in (3, 6, 9))
    natural = jnp.zeros((8, LANES), jnp.float32)
    for r in range(MODES):
        block = jnp.concatenate([loads[r], jnp.zeros((4, 4), jnp.float32)], axis=0)
        block = jnp.concatenate([block, jnp.zeros((8, LANES - 4), jnp.float32)], axis=1)
        here = (off >= 0) & (off < 12) & (off - 3 * y == r) & (x < 4)
        natural = natural + jnp.where(here, lane_gather(block, y), 0.0)
    natural = jnp.broadcast_to(jnp.sum(natural, axis=0, keepdims=True), (8, LANES))
    owner_row = jnp.concatenate([owner[...], jnp.zeros((1, LANES - BLOCK), jnp.int32)], axis=1)
    flat = lane_gather(natural, jnp.broadcast_to(owner_row, (8, LANES)))[0:1]
    hit = (jnp.broadcast_to(owner_row, (E, E)).T == lane) & (at < BLOCK)
    inverse = jnp.sum(jnp.where(hit, at, 0), axis=0, keepdims=True).astype(jnp.float32)
    lane1 = lax.broadcasted_iota(jnp.int32, (1, LANES), 1)
    row = jnp.where(lane1 < BLOCK, flat, pltpu.roll(jnp.broadcast_to(inverse, (8, LANES)), BLOCK, 1)[0:1])
    three = lambda first, step: [kept[first + step * r] for r in range(MODES)]
    edges = (
        three(TMW, 1),
        three(M + 1, 4) + [kept[LOAD_E]],
        three(TMS, 1),
        three(M + 3, 4) + [kept[LOAD_N]],
    )
    send_rows(row, edges, out)


def pack_constants(arrived, maps, kept, pack):
    nb_tw, nb_e, nb_ts, nb_n = arrived_edges(arrived, EDGES_SETUP)
    for i in range(LOAD_E):
        pack[i] = kept[i]
    for r in range(MODES):
        pack[NB_TMW + r] = nb_tw[r]
        pack[NB_ME + r] = nb_e[r]
        pack[NB_TMS + r] = nb_ts[r]
        pack[NB_MN + r] = nb_n[r]
    local = Local(maps, pack)
    none = jnp.zeros((SUB, LANES), jnp.float32)
    load = (none, kept[LOAD_E], none, kept[LOAD_N])
    target = local.cross(load, (none, none), (none, nb_e[MODES], none, nb_n[MODES]))
    for side in range(4):
        pack[TARGET + side] = target[side]
    return local, local.absorb(none, target)


W, T, LAM, G0, COARSE, P1, G1, MOVED = 0, 4, 6, 8, 12, 13, 15, 17


def product_out(local, total, state, w, t, out_row):
    keep(state, *w, *t)
    local.send(total, ([t[0]], [w[1]], [t[1]], [w[3]]), out_row)


def image_of(local, arrived, state):
    w = [state[W + i] for i in range(4)]
    near = [arrays[0] for arrays in arrived_edges(arrived, EDGES)]
    return w, local.cross(w, [state[T], state[T + 1]], near)


def first_kernel(arrived, maps, kept, dual_ops, out_row, state, pack, *rest):
    operators = Operators(dual_ops, *rest)
    local, entries = pack_constants(arrived, maps, kept, pack)
    u = local.lift(from_peers(arrived))
    w, t = local.dual(u, operators, False)
    product_out(local, entries - local.contributions(w, t), state, w, t, out_row)
    state[LAM] = u[1]
    state[LAM + 1] = u[3]


def second_kernel(arrived, maps, pack, dual_ops, before, out_row, state, *rest):
    operators = Operators(dual_ops, *rest)
    local = Local(maps, pack)
    row = from_peers(arrived)
    _, image = image_of(local, arrived, before)
    lifted = local.lift(row)
    g = [pack[TARGET + i] - image[i] - lifted[i] for i in range(4)]
    w, t = local.dual(g, operators, False)
    total = local.contributions(w, t)
    total = local.put(total, g[1] * g[1] + g[3] * g[3], AT_SCALAR)
    total = local.put(total, sum(g[i] * w[i] for i in range(4)), AT_SCALAR + 1)
    product_out(local, total, state, w, t, out_row)
    state[LAM] = before[LAM]
    state[LAM + 1] = before[LAM + 1]
    for i in range(4):
        state[G0 + i] = g[i]
    state[COARSE] = jnp.broadcast_to(row, (SUB, LANES))


def third_kernel(arrived, maps, pack, dual_ops, before, sums, out_row, state, *rest):
    operators = Operators(dual_ops, *rest)
    local = Local(maps, pack)
    alpha = scalar(sums, 0) / scalar(sums, 1)
    row = from_peers(arrived)
    w1, image = image_of(local, arrived, before)
    lifted = local.lift(row)
    p = [image[i] - lifted[i] for i in range(4)]
    g0 = [before[G0 + i] for i in range(4)]
    g = [g0[i] - alpha * p[i] for i in range(4)]
    w, t = local.dual(g, operators, True)
    total = local.contributions(w, t)
    total = local.put(total, g[1] * g[1] + g[3] * g[3], AT_SCALAR)
    total = local.put(total, sum(g[i] * w[i] for i in range(4)), AT_SCALAR + 1)
    total = local.put(total, sum(g0[i] * w[i] + g[i] * w1[i] for i in range(4)), AT_SCALAR + 2)
    product_out(local, total, state, w, t, out_row)
    state[LAM] = before[LAM] + alpha * g0[1]
    state[LAM + 1] = before[LAM + 1] + alpha * g0[3]
    for i in range(4):
        state[G0 + i] = g0[i]
    state[COARSE] = before[COARSE] - alpha * row
    for i, side in ((0, 1), (1, 3)):
        state[P1 + i] = p[side]
        state[G1 + i] = g[side]
    state[MOVED] = jnp.broadcast_to(row, (SUB, LANES))


def last_kernel(arrived, maps, pack, before, sums, sums_next, lam_out, g_out, amplitudes):
    local = Local(maps, pack)
    beta = scalar(sums_next, 0) / scalar(sums, 0)
    curve = scalar(sums_next, 1) + beta * (scalar(sums_next, 2) + beta * scalar(sums, 1))
    alpha = scalar(sums_next, 0) / curve
    row = from_peers(arrived)
    _, image = image_of(local, arrived, before)
    lifted = local.lift(row)
    for i, side in ((0, 1), (1, 3)):
        p = image[side] - lifted[side] + beta * before[P1 + i]
        g_out[:, i, :] = before[G1 + i] - alpha * p
        lam_out[:, i, :] = before[LAM + i] + alpha * (before[G1 + i] + beta * before[G0 + side])
    a = alpha * (row + beta * before[MOVED]) - before[COARSE]
    x = lax.broadcasted_iota(jnp.int32, (SUB, LANES), 0)
    for r in range(MODES):
        at = jnp.minimum(12 * x + 3 * local.lane + r, 127)
        amplitudes[r] = lane_gather(a, at)[:4, :4]


def third_of(lane, base):
    off = lane - base
    return sum((off >= c).astype(jnp.int32) for c in (3, 6, 9)), off


def coarse_body(entries, owner, inverse, factor, out, first=False):
    lane = lax.broadcasted_iota(jnp.int32, (PEERS, LANES), 1)
    group = sum((lane >= c).astype(jnp.int32) for c in (12, 24, 36))
    within = lane - 12 * group
    clip = lambda index: jnp.clip(index, 0, LANES - 1)
    total = entries
    if not first:
        from_e = up(lane_gather(entries, clip(lane + 12)), 8)
        from_w = down(lane_gather(entries, clip(lane + 60)), 8)
        from_n = up(lane_gather(entries, clip(63 + 3 * group + within)), 1)
        from_s = down(lane_gather(entries, clip(84 + 3 * group + within)), 1)
        total = total + jnp.where(lane >= 36, from_e, 0.0) + jnp.where(lane < 12, from_w, 0.0)
        total = total + jnp.where(within >= 9, from_n, 0.0) + jnp.where(within < 3, from_s, 0.0)
    placed = lane_gather(total, owner)
    q = lax.broadcasted_iota(jnp.int32, (8, LANES), 0)
    within = lax.bitwise_and(lax.broadcasted_iota(jnp.int32, (8, LANES), 1) - BLOCK * q, LANES - 1)
    column = jnp.where(within < BLOCK, lax.shift_right_logical(BLOCK * q + within, 7), -1)
    here = [column == j for j in range(3)]
    groups = PEERS // 8
    tile = lambda g, j: factor[:, (3 * g + j) * LANES : (3 * g + j + 1) * LANES]
    y = jnp.zeros((BLOCK, LANES), jnp.float32)
    for g in range(groups):
        rows = placed[8 * g : 8 * g + 8]
        for j in range(3):
            y = y + tile(g, j) * jnp.sum(jnp.where(here[j], rows, 0.0), axis=0, keepdims=True)
    y = jnp.broadcast_to(jnp.sum(y, axis=1, keepdims=True), (BLOCK, LANES))
    spread = []
    for g in range(groups):
        z = [jnp.sum(tile(g, j) * y, axis=0, keepdims=True) for j in range(3)]
        spread.append(jnp.where(here[0], z[0], jnp.where(here[1], z[1], z[2])))
    natural = lane_gather(jnp.concatenate(spread, axis=0), inverse)
    g3, off3 = third_of(lane, AT_S)
    g4, off4 = third_of(lane, AT_N)
    at_w = down(lane_gather(natural, clip(lane - 12)), 8)
    at_e = up(lane_gather(natural, clip(lane - 60)), 8)
    at_s = down(lane_gather(natural, clip(9 * g3 + 9 + off3)), 1)
    at_n = up(lane_gather(natural, clip(9 * g4 + off4)), 1)
    edge = jnp.where(lane < AT_E, at_w, jnp.where(lane < AT_S, at_e, jnp.where(lane < AT_N, at_s, at_n)))
    edges = pass_on(entries, lane, EDGES_SETUP if first else EDGES)
    out[...] = jnp.where(lane < AT_W, natural, jnp.where(lane < AT_EDGE, edge, edges))


def places():
    lane = lax.broadcasted_iota(jnp.int32, (PEERS, LANES), 1)
    return lane, BLOCK * lax.bitwise_and(lax.broadcasted_iota(jnp.int32, (PEERS, LANES), 0), 7)


def coarse_first_kernel(entries, factor, out, inverse_out):
    lane, start = places()
    got = entries[...]
    inverse = jnp.where(lane < BLOCK, pltpu.roll(got, LANES - BLOCK, 1).astype(jnp.int32), lane)
    inverse = lax.bitwise_and(inverse + start, LANES - 1)
    inverse_out[...] = inverse
    coarse_body(got, lax.bitwise_and(lane - start, LANES - 1), inverse, factor, out, True)


def owner_kernel(inverse, owner_out):
    lane, start = places()
    places_of = lax.bitwise_and(inverse[...] - start, LANES - 1)
    owner = lane
    for k in range(BLOCK):
        owner = jnp.where(places_of[:, k : k + 1] == lane, k, owner)
    owner_out[...] = lane_gather(owner, lax.bitwise_and(lane - start, LANES - 1))


def coarse_kernel(entries, owner, inverse, factor, out, sums):
    got = entries[...]
    sums[...] = jnp.sum(got, axis=0, keepdims=True)
    coarse_body(got, owner[...], inverse[...], factor, out, False)


def f32(*shape):
    return jax.ShapeDtypeStruct(shape, jnp.float32)


def i32(*shape):
    return jax.ShapeDtypeStruct(shape, jnp.int32)


def call(kernel, outs, *args, operators=None):
    specs = [pl.BlockSpec(memory_space=pltpu.HBM) if i == operators else pl.BlockSpec() for i in range(len(args))]
    scratch = []
    if operators is not None:
        scratch = [pltpu.VMEM((SUB, 4 * E, 4 * E), jnp.bfloat16), pltpu.SemaphoreType.DMA((SUB,))]
    return pl.pallas_call(
        kernel,
        out_shape=outs,
        in_specs=specs,
        out_specs=tuple(pl.BlockSpec() for _ in outs),
        scratch_shapes=scratch,
        compiler_params=pltpu.CompilerParams(vmem_limit_bytes=(24 if operators is None else 56) * 1024 * 1024),
    )(*args)


def exchange(rows):
    return lax.all_to_all(rows, ALL, split_axis=0, concat_axis=0, tiled=True)


def shards(dual_ops, dual_load, mode_images, mode_loads, coarse_factor, west_map, south_map, mode_owner):
    rows, row, indices = f32(PEERS, LANES), f32(1, LANES), i32(PEERS, LANES)
    sent, maps, kept = call(
        start_kernel,
        (rows, i32(4, SUB, E), f32(KEPT, SUB, E)),
        mode_loads.transpose(2, 0, 1),
        mode_owner.reshape(1, BLOCK),
        west_map,
        south_map,
        mode_images.transpose(0, 2, 1, 3),
        dual_load,
    )
    partial, inverse = call(coarse_first_kernel, (rows, indices), exchange(sent), coarse_factor)
    arrived = exchange(partial)
    (owner,) = call(owner_kernel, (indices,), inverse)

    def solve(sent):
        partial, sums = call(coarse_kernel, (rows, row), exchange(sent), owner, inverse, coarse_factor)
        return exchange(partial), sums

    sent, state, pack = call(
        first_kernel, (rows, f32(8, SUB, E), f32(PACKED, SUB, E)), arrived, maps, kept, dual_ops, operators=3
    )
    arrived, _ = solve(sent)
    sent, state = call(
        second_kernel, (rows, f32(13, SUB, E)), arrived, maps, pack, dual_ops, state, operators=3
    )
    arrived, sums = solve(sent)
    sent, state = call(
        third_kernel, (rows, f32(18, SUB, E)), arrived, maps, pack, dual_ops, state, sums, operators=3
    )
    arrived, sums_next = solve(sent)
    lam, gradient, amplitudes = call(
        last_kernel,
        (f32(SUB, 2, E), f32(SUB, 2, E), f32(MODES, 4, 4)),
        arrived,
        maps,
        pack,
        state,
        sums,
        sums_next,
    )
    return lam.reshape(4, 4, 2, E), gradient.reshape(4, 4, 2, E), amplitudes.transpose(1, 2, 0)


def solution(mesh):
    placed = (
        P(GX, GY, None, None),
        P(GX, GY, None, None),
        P(GX, GY, None, None),
        P(GX, GY, None),
        P(ALL, None),
        P(GX, GY, None),
        P(GX, GY, None),
        P(ALL),
    )
    return jax.shard_map(
        shards,
        mesh=mesh,
        in_specs=placed,
        out_specs=(P(GX, GY, None, None), P(GX, GY, None, None), P(GX, GY, None)),
        check_vma=False,
    )
```

time: 296 us -> 194 us (0.66)
  the two profiles are of different devices: /device:TPU:30 before, /device:TPU:1 now
where the time goes in v1:
time: 194 us
  blocking collectives  142 us (73%)
  Pallas kernels  27 us (14%)
  waiting for transfers between devices  11 us (6%)
  local copies, waits for them, and re-layouts  7.6 us (4%)
  starting transfers between devices  5.45 us (3%)
    all_to_all x7, blocking collectives, exchange(): return lax.all_to_all(rows, ALL, split_axis=0, concat_axis=0, tiled=True)  142 us
    pallas_call x10, Pallas kernels, call(): pl.pallas_call(kernel, out_shape=outs, in_specs=specs, out_specs=tuple((p...  27 us
    all_to_all x1, waiting for transfers between devices, exchange(): return lax.all_to_all(rows, ALL, split_axis=0, concat_axis=0, tiled=True)  11 us
    unnamed x30, local copies, waits for them, and re-layouts  7.6 us
    all_to_all x1, starting transfers between devices, exchange(): return lax.all_to_all(rows, ALL, split_axis=0, concat_axis=0, tiled=True)  5.45 us
  transfers between devices with their start and end apart: 1, of which 1 were waited for; matrix products, arithmetic and copies ran while one was open for 0% of the time, Pallas kernels for 1%

profile of v1, /device:TPU:1, one launch (start us, length us, event | category | flops | bytes accessed | tf_op | source)
XLA Modules:
  0.0 193.5 jit_solution(14663678962394200609)
XLA Ops:
  0.6 0.0 copy-start.7
  0.6 0.9 copy-done.7
  1.5 0.0 copy-start.8
  1.5 0.7 copy-done.8
  2.2 0.0 copy-start.9
  2.2 0.7 copy-done.9
  2.9 0.0 copy-start.10
  2.9 0.7 copy-done.10
  3.6 0.0 copy-start.11
  3.6 0.7 copy-done.11
  4.3 0.0 copy-start.14
  4.3 0.7 copy-done.14
  5.0 1.0 shard_map.103
  6.0 0.0 copy-start.3
  6.0 0.0 copy-start.5
  6.0 28.3 %all_to_all.88 = f32[256,1,128]{2,1,0:T(1,128)S(1)} all-to-all(f32[256,1,128]{2,1,0:T(1,128)S(1)} %bitcast.44), channel_id=1, replica_groups=mesh['gx'=32,'gy'=8] {'gx','gy'}, dimensions={0} | all-to-all | bytes 262144 | tf_op jit(solution)/shard_map/all_to_all | solution.py:476
  34.3 0.0 copy-done.3
  34.3 0.0 copy-done.5
  34.3 0.0 copy-start
  34.3 1.7 copy-done
  36.0 0.0 copy-start.1
  36.0 0.9 shard_map.104
  36.9 19.0 %all_to_all.89 = f32[256,1,128]{2,1,0:T(1,128)} all-to-all(f32[256,1,128]{2,1,0:T(1,128)S(1)} %bitcast.45), channel_id=1, replica_groups=mesh['gx'=32,'gy'=8] {'gx','gy'}, dimensions={0} | all-to-all | bytes 262144 | tf_op jit(solution)/shard_map/all_to_all | solution.py:476
  55.9 6.0 %shard_map.105 = (f32[256,128]{1,0:T(8,128)}, f32[8,16,128]{2,1,0:T(8,128)}, f32[36,16,128]{2,1,0:T(8,128)}) custom-call(f32[256,128]{1,0:T(8,128)} %bitcast.51, s32[4,16,128]{2,1,0:T(8,128)} %copy-done.3, f32[22,16,128]{2,1,0:T(8,128)} %copy-done.5, bf16[4,4,512,512]{3,2,1,0:T(8,128)(2,1)} %dual_ops.5), custom_call_target="tpu_custom_call" | custom-call | tf_op jit(solution)/shard_map/pallas_call | solution.py:465
  61.9 5.4 %all-to-all-start.2 = ((f32[256,1,128]{2,1,0:T(1,128)}), f32[256,1,128]{2,1,0:T(1,128)S(1)}, u32[]{:S(2)}, u32[]{:S(2)}) async-start(f32[256,1,128]{2,1,0:T(1,128)} %bitcast.54), calls=%async_computation.2 | async-start | bytes 262144 | tf_op jit(solution)/shard_map/all_to_all | solution.py:476
  67.4 1.9 shard_map.106.owner
  69.3 11.0 %all-to-all-done.2 = f32[256,1,128]{2,1,0:T(1,128)S(1)} async-done(((f32[256,1,128]{2,1,0:T(1,128)}), f32[256,1,128]{2,1,0:T(1,128)S(1)}, u32[]{:S(2)}, u32[]{:S(2)}) %all-to-all-start.2) | async-done | bytes 131104 | tf_op jit(solution)/shard_map/all_to_all | solution.py:476
  80.3 0.0 copy-done.1
  80.3 1.5 shard_map.107
  81.9 18.9 %all_to_all.90 = f32[256,1,128]{2,1,0:T(1,128)} all-to-all(f32[256,1,128]{2,1,0:T(1,128)S(1)} %bitcast.46), channel_id=1, replica_groups=mesh['gx'=32,'gy'=8] {'gx','gy'}, dimensions={0} | all-to-all | bytes 262144 | tf_op jit(solution)/shard_map/all_to_all | solution.py:476
  100.8 6.0 %shard_map.108 = (f32[256,128]{1,0:T(8,128)}, f32[13,16,128]{2,1,0:T(8,128)}) custom-call(f32[256,128]{1,0:T(8,128)} %bitcast.53, s32[4,16,128]{2,1,0:T(8,128)} %copy-done.3, f32[36,16,128]{2,1,0:T(8,128)} %get-tuple-element.30.pack, bf16[4,4,512,512]{3,2,1,0:T(8,128)(2,1)} %dual_ops.5, f32[8,16,128]{2,1,0:T(8,128)} %get-tuple-element.31.before), custom_call_target="tpu_custom_call" | custom-call | tf_op jit(solution)/shard_map/pallas_call | solution.py:465
  106.9 0.0 copy-start.2
  106.9 0.0 copy-start.4
  106.9 19.3 %all_to_all.91 = f32[256,1,128]{2,1,0:T(1,128)S(1)} all-to-all(f32[256,1,128]{2,1,0:T(1,128)} %bitcast.55), channel_id=1, replica_groups=mesh['gx'=32,'gy'=8] {'gx','gy'}, dimensions={0} | all-to-all | bytes 262144 | tf_op jit(solution)/shard_map/all_to_all | solution.py:476
  126.2 1.1 shard_map.109
  127.3 0.0 copy-start.12
  127.3 19.1 %all_to_all.92 = f32[256,1,128]{2,1,0:T(1,128)} all-to-all(f32[256,1,128]{2,1,0:T(1,128)S(1)} %bitcast.47), channel_id=1, replica_groups=mesh['gx'=32,'gy'=8] {'gx','gy'}, dimensions={0} | all-to-all | bytes 262144 | tf_op jit(solution)/shard_map/all_to_all | solution.py:476
  146.3 0.0 copy-done.12
  146.3 6.3 %shard_map.110 = (f32[256,128]{1,0:T(8,128)}, f32[18,16,128]{2,1,0:T(8,128)}) custom-call(f32[256,128]{1,0:T(8,128)} %bitcast.52, s32[4,16,128]{2,1,0:T(8,128)} %copy-done.3, f32[36,16,128]{2,1,0:T(8,128)} %get-tuple-element.30.pack, bf16[4,4,512,512]{3,2,1,0:T(8,128)(2,1)} %dual_ops.5, f32[13,16,128]{2,1,0:T(8,128)} %get-tuple-element.34.before, ...), custom_call_target="tpu_custom_call" | custom-call | tf_op jit(solution)/shard_map/pallas_call | solution.py:465
  152.7 18.8 %all_to_all.93 = f32[256,1,128]{2,1,0:T(1,128)S(1)} all-to-all(f32[256,1,128]{2,1,0:T(1,128)} %bitcast.56), channel_id=1, replica_groups=mesh['gx'=32,'gy'=8] {'gx','gy'}, dimensions={0} | all-to-all | bytes 262144 | tf_op jit(solution)/shard_map/all_to_all | solution.py:476
  171.5 1.1 shard_map.111
  172.6 18.2 %all_to_all.94 = f32[256,1,128]{2,1,0:T(1,128)S(1)} all-to-all(f32[256,1,128]{2,1,0:T(1,128)S(1)} %bitcast.43), channel_id=1, replica_groups=mesh['gx'=32,'gy'=8] {'gx','gy'}, dimensions={0} | all-to-all | bytes 262144 | tf_op jit(solution)/shard_map/all_to_all | solution.py:476
  190.8 0.0 copy-done.2
  190.8 0.0 copy-done.4
  190.8 0.0 copy-start.6
  190.8 0.9 copy-done.6
  191.8 0.7 copy-done.13
  192.4 1.1 shard_map.112
  (1 shorter events, 0.0 us)
Async XLA Ops:
  0.6 0.9 copy-start.7
  1.5 0.7 copy-start.8
  2.2 0.7 copy-start.9
  2.9 0.7 copy-start.10
  3.6 0.7 copy-start.11
  4.3 0.7 copy-start.14
  6.0 28.3 %copy-start.3 = (s32[4,16,128]{2,1,0:T(8,128)}, s32[4,16,128]{2,1,0:T(8,128)S(1)}, u32[]{:S(2)}) copy-start(s32[4,16,128]{2,1,0:T(8,128)S(1)} %get-tuple-element.25.maps) | copy-start | bytes 98308
  6.0 28.3 %copy-start.5 = (f32[22,16,128]{2,1,0:T(8,128)}, f32[22,16,128]{2,1,0:T(8,128)S(1)}, u32[]{:S(2)}) copy-start(f32[22,16,128]{2,1,0:T(8,128)S(1)} %get-tuple-element.26.kept) | copy-start | bytes 540676
  34.3 1.7 copy-start
  36.0 44.4 %copy-start.1 = (f32[48,12288]{1,0:T(8,128)S(1)}, f32[48,12288]{1,0:T(8,128)}, u32[]{:S(2)}) copy-start(f32[48,12288]{1,0:T(8,128)} %factor.7) | copy-start | bytes 7077892
  61.9 18.4 %all-to-all-start.2 = ((f32[256,1,128]{2,1,0:T(1,128)}), f32[256,1,128]{2,1,0:T(1,128)S(1)}, u32[]{:S(2)}, u32[]{:S(2)}) async-start(f32[256,1,128]{2,1,0:T(1,128)} %bitcast.54), calls=%async_computation.2 | async-start | bytes 262144 | tf_op jit(solution)/shard_map/all_to_all | solution.py:476
  106.9 84.0 %copy-start.2 = (f32[36,16,128]{2,1,0:T(8,128)S(1)}, f32[36,16,128]{2,1,0:T(8,128)}, u32[]{:S(2)}) copy-start(f32[36,16,128]{2,1,0:T(8,128)} %get-tuple-element.30.pack) | copy-start | bytes 884740
  106.9 84.0 %copy-start.4 = (s32[4,16,128]{2,1,0:T(8,128)S(1)}, s32[4,16,128]{2,1,0:T(8,128)}, u32[]{:S(2)}) copy-start(s32[4,16,128]{2,1,0:T(8,128)} %copy-done.3) | copy-start | bytes 98308
  127.3 19.1 %copy-start.12 = (f32[1,128]{1,0:T(1,128)}, f32[1,128]{1,0:T(1,128)S(1)}, u32[]{:S(2)}) copy-start(f32[1,128]{1,0:T(1,128)S(1)} %get-tuple-element.35.sums) | copy-start | bytes 1540
  190.8 0.9 copy-start.6
  191.8 0.7 copy-start.13

commit v2 on v1

--- a/solution.py
+++ b/solution.py
@@ -32,13 +32,14 @@
 
 
 KEEP_W, KEEP_S, M, TMW, TMS, NB_TMW, NB_ME, NB_TMS, NB_MN, TARGET = 0, 1, 2, 14, 17, 20, 23, 26, 29, 32
-PACKED = 36
+MAPS, PACKED = 36, 40
 WMAP, SMAP, WINV, SINV = range(4)
 
 
 class Local:
-    def __init__(self, maps, pack):
-        self.maps, self.pack = maps, pack
+    def __init__(self, pack):
+        self.pack = pack
+        self.maps = [pack[MAPS + i].astype(jnp.int32) for i in range(4)]
         s = lax.broadcasted_iota(jnp.int32, (SUB, LANES), 0)
         self.lane = lax.broadcasted_iota(jnp.int32, (SUB, LANES), 1)
         self.s, self.x, self.y = s, lax.shift_right_logical(s, 2), lax.bitwise_and(s, 3)
@@ -124,7 +125,7 @@
         row = lax.broadcasted_iota(jnp.int32, (SUB, 4 * E), 0)
         out = jnp.zeros((SUB, 4 * E), jnp.float32)
         for k in range(SUB):
-            product = jnp.dot(left, operators.get(k), preferred_element_type=jnp.float32)
+            product = operators.times(k, left)
             if precise:
                 product = product[:SUB] + product[SUB:]
             out = jnp.where(row == k, product, out)
@@ -145,9 +146,9 @@
             copy.start()
             self.copies.append(copy)
 
-    def get(self, k):
+    def times(self, k, left):
         self.copies[k].wait()
-        return self.held[k]
+        return jnp.dot(left, self.held[k], preferred_element_type=jnp.float32)
 
 
 EDGE_ROWS = ([0, 1, 2, 3], [12, 13, 14, 15], [0, 4, 8, 12], [3, 7, 11, 15])
@@ -211,21 +212,23 @@
         ref[i] = jnp.broadcast_to(part, (SUB, LANES))
 
 
-LOAD_E, LOAD_N, KEPT = 20, 21, 22
-
-
-def start_kernel(loads, owner, west_map, south_map, images, load, out, maps, kept):
+LOAD_E, LOAD_N, KEPT_MAPS, KEPT = 20, 21, 22, 26
+
+
+def start_kernel(loads, owner, west_map, south_map, images, load, out, kept):
     lane = lax.broadcasted_iota(jnp.int32, (E, E), 1)
     at = lax.broadcasted_iota(jnp.int32, (E, E), 0)
+    inverses = []
     for source, direct, inverse in ((west_map, WMAP, WINV), (south_map, SMAP, SINV)):
         rows = jnp.concatenate([source[x] for x in range(4)], axis=0)
-        maps[direct] = rows
+        kept[KEPT_MAPS + direct] = rows.astype(jnp.float32)
         columns = jnp.concatenate([rows, jnp.zeros((E - SUB, E), jnp.int32)], axis=0).T
         found = []
         for k in range(SUB):
             hit = columns[:, k : k + 1] == lane
             found.append(jnp.sum(jnp.where(hit, at, 0), axis=0, keepdims=True))
-        maps[inverse] = jnp.concatenate(found, axis=0)
+        inverses.append(jnp.concatenate(found, axis=0))
+        kept[KEPT_MAPS + inverse] = inverses[-1].astype(jnp.float32)
     s = lax.broadcasted_iota(jnp.int32, (SUB, LANES), 0)
     first_x, first_y = lax.axis_index(GX) == 0, lax.axis_index(GY) == 0
     kept[KEEP_W] = jnp.where(first_x & (s < 4), 0.0, 1.0)
@@ -234,8 +237,8 @@
         whole = jnp.concatenate([images[x, r] for x in range(4)], axis=0)
         for side in range(4):
             kept[M + 4 * r + side] = whole[:, side * E : (side + 1) * E]
-        kept[TMW + r] = lane_gather(whole[:, :E], maps[WINV])
-        kept[TMS + r] = lane_gather(whole[:, 2 * E : 3 * E], maps[SINV])
+        kept[TMW + r] = lane_gather(whole[:, :E], inverses[0])
+        kept[TMS + r] = lane_gather(whole[:, 2 * E : 3 * E], inverses[1])
     kept[LOAD_E] = jnp.concatenate([load[k // 4, k % 4, 0:1, :] for k in range(SUB)], axis=0)
     kept[LOAD_N] = jnp.concatenate([load[k // 4, k % 4, 1:2, :] for k in range(SUB)], axis=0)
 
@@ -266,16 +269,18 @@
     send_rows(row, edges, out)
 
 
-def pack_constants(arrived, maps, kept, pack):
+def pack_constants(arrived, kept, pack):
     nb_tw, nb_e, nb_ts, nb_n = arrived_edges(arrived, EDGES_SETUP)
     for i in range(LOAD_E):
         pack[i] = kept[i]
+    for i in range(4):
+        pack[MAPS + i] = kept[KEPT_MAPS + i]
     for r in range(MODES):
         pack[NB_TMW + r] = nb_tw[r]
         pack[NB_ME + r] = nb_e[r]
         pack[NB_TMS + r] = nb_ts[r]
         pack[NB_MN + r] = nb_n[r]
-    local = Local(maps, pack)
+    local = Local(pack)
     none = jnp.zeros((SUB, LANES), jnp.float32)
     load = (none, kept[LOAD_E], none, kept[LOAD_N])
     target = local.cross(load, (none, none), (none, nb_e[MODES], none, nb_n[MODES]))
@@ -298,9 +303,9 @@
     return w, local.cross(w, [state[T], state[T + 1]], near)
 
 
-def first_kernel(arrived, maps, kept, dual_ops, out_row, state, pack, *rest):
+def first_kernel(arrived, kept, dual_ops, out_row, state, pack, *rest):
     operators = Operators(dual_ops, *rest)
-    local, entries = pack_constants(arrived, maps, kept, pack)
+    local, entries = pack_constants(arrived, kept, pack)
     u = local.lift(from_peers(arrived))
     w, t = local.dual(u, operators, False)
     product_out(local, entries - local.contributions(w, t), state, w, t, out_row)
@@ -308,9 +313,9 @@
     state[LAM + 1] = u[3]
 
 
-def second_kernel(arrived, maps, pack, dual_ops, before, out_row, state, *rest):
+def second_kernel(arrived, pack, dual_ops, before, out_row, state, *rest):
     operators = Operators(dual_ops, *rest)
-    local = Local(maps, pack)
+    local = Local(pack)
     row = from_peers(arrived)
     _, image = image_of(local, arrived, before)
     lifted = local.lift(row)
@@ -327,9 +332,9 @@
     state[COARSE] = jnp.broadcast_to(row, (SUB, LANES))
 
 
-def third_kernel(arrived, maps, pack, dual_ops, before, sums, out_row, state, *rest):
+def third_kernel(arrived, pack, dual_ops, before, sums, out_row, state, *rest):
     operators = Operators(dual_ops, *rest)
-    local = Local(maps, pack)
+    local = Local(pack)
     alpha = scalar(sums, 0) / scalar(sums, 1)
     row = from_peers(arrived)
     w1, image = image_of(local, arrived, before)
@@ -354,8 +359,8 @@
     state[MOVED] = jnp.broadcast_to(row, (SUB, LANES))
 
 
-def last_kernel(arrived, maps, pack, before, sums, sums_next, lam_out, g_out, amplitudes):
-    local = Local(maps, pack)
+def last_kernel(arrived, pack, before, sums, sums_next, lam_out, g_out, amplitudes):
+    local = Local(pack)
     beta = scalar(sums_next, 0) / scalar(sums, 0)
     curve = scalar(sums_next, 1) + beta * (scalar(sums_next, 2) + beta * scalar(sums, 1))
     alpha = scalar(sums_next, 0) / curve
@@ -443,9 +448,10 @@
     owner_out[...] = lane_gather(owner, lax.bitwise_and(lane - start, LANES - 1))
 
 
-def coarse_kernel(entries, owner, inverse, factor, out, sums):
+def coarse_kernel(entries, owner, inverse, factor, out, *sums):
     got = entries[...]
-    sums[...] = jnp.sum(got, axis=0, keepdims=True)
+    for ref in sums:
+        ref[...] = jnp.sum(got, axis=0, keepdims=True)
     coarse_body(got, owner[...], inverse[...], factor, out, False)
 
 
@@ -457,19 +463,31 @@
     return jax.ShapeDtypeStruct(shape, jnp.int32)
 
 
-def call(kernel, outs, *args, operators=None):
+def call(kernel, outs, *args, operators=None, megabytes=16):
     specs = [pl.BlockSpec(memory_space=pltpu.HBM) if i == operators else pl.BlockSpec() for i in range(len(args))]
     scratch = []
     if operators is not None:
-        scratch = [pltpu.VMEM((SUB, 4 * E, 4 * E), jnp.bfloat16), pltpu.SemaphoreType.DMA((SUB,))]
+        megabytes = 50
+        scratch = [
+            pltpu.VMEM((SUB, 4 * E, 4 * E), jnp.bfloat16),
+            pltpu.SemaphoreType.DMA((SUB,)),
+        ]
     return pl.pallas_call(
         kernel,
         out_shape=outs,
         in_specs=specs,
         out_specs=tuple(pl.BlockSpec() for _ in outs),
         scratch_shapes=scratch,
-        compiler_params=pltpu.CompilerParams(vmem_limit_bytes=(24 if operators is None else 56) * 1024 * 1024),
+        compiler_params=pltpu.CompilerParams(vmem_limit_bytes=megabytes * 1024 * 1024),
     )(*args)
+
+
+def settle_kernel(value, out):
+    out[...] = value[...]
+
+
+def after(first, *values):
+    return lax.optimization_barrier((first, values))
 
 
 def exchange(rows):
@@ -478,41 +496,43 @@
 
 def shards(dual_ops, dual_load, mode_images, mode_loads, coarse_factor, west_map, south_map, mode_owner):
     rows, row, indices = f32(PEERS, LANES), f32(1, LANES), i32(PEERS, LANES)
-    sent, maps, kept = call(
+    sent, kept = call(
         start_kernel,
-        (rows, i32(4, SUB, E), f32(KEPT, SUB, E)),
+        (rows, f32(KEPT, SUB, E)),
         mode_loads.transpose(2, 0, 1),
         mode_owner.reshape(1, BLOCK),
         west_map,
         south_map,
         mode_images.transpose(0, 2, 1, 3),
         dual_load,
+        megabytes=60,
     )
     partial, inverse = call(coarse_first_kernel, (rows, indices), exchange(sent), coarse_factor)
+    partial, (kept,) = after(partial, kept)
     arrived = exchange(partial)
+    (kept,) = call(settle_kernel, (f32(KEPT, SUB, E),), kept)
     (owner,) = call(owner_kernel, (indices,), inverse)
 
-    def solve(sent):
-        partial, sums = call(coarse_kernel, (rows, row), exchange(sent), owner, inverse, coarse_factor)
-        return exchange(partial), sums
+    def solve(sent, *sums):
+        partial, *sums = call(coarse_kernel, (rows, *sums), exchange(sent), owner, inverse, coarse_factor)
+        return exchange(partial), *sums
 
     sent, state, pack = call(
-        first_kernel, (rows, f32(8, SUB, E), f32(PACKED, SUB, E)), arrived, maps, kept, dual_ops, operators=3
-    )
-    arrived, _ = solve(sent)
+        first_kernel, (rows, f32(8, SUB, E), f32(PACKED, SUB, E)), arrived, kept, dual_ops, operators=2
+    )
+    (arrived,) = solve(sent)
     sent, state = call(
-        second_kernel, (rows, f32(13, SUB, E)), arrived, maps, pack, dual_ops, state, operators=3
-    )
-    arrived, sums = solve(sent)
+        second_kernel, (rows, f32(13, SUB, E)), arrived, pack, dual_ops, state, operators=2
+    )
+    arrived, sums = solve(sent, row)
     sent, state = call(
-        third_kernel, (rows, f32(18, SUB, E)), arrived, maps, pack, dual_ops, state, sums, operators=3
-    )
-    arrived, sums_next = solve(sent)
+        third_kernel, (rows, f32(18, SUB, E)), arrived, pack, dual_ops, state, sums, operators=2
+    )
+    arrived, sums_next = solve(sent, row)
     lam, gradient, amplitudes = call(
         last_kernel,
         (f32(SUB, 2, E), f32(SUB, 2, E), f32(MODES, 4, 4)),
         arrived,
-        maps,
         pack,
         state,
         sums,

time: 194 us -> 182 us (0.938)
  blocking collectives: 142 us -> 119 us
  waiting for transfers between devices: 11 us -> 23 us
  starting transfers between devices: 5.45 us -> 11.1 us
  local copies, waits for them, and re-layouts: 7.6 us -> 2.59 us
  Pallas kernels: 27 us -> 24.4 us
    all_to_all x7 -> x6, blocking collectives: 142 us -> 119 us  [exchange(): return lax.all_to_all(rows, ALL, split_axis=0, concat_axis=0, tiled=True)]
    all_to_all x1 -> x2, waiting for transfers between devices: 11 us -> 23 us  [exchange(): return lax.all_to_all(rows, ALL, split_axis=0, concat_axis=0, tiled=True)]
    all_to_all x1 -> x2, starting transfers between devices: 5.45 us -> 11.1 us  [exchange(): return lax.all_to_all(rows, ALL, split_axis=0, concat_axis=0, tiled=True)]
    unnamed x30 -> x6, local copies, waits for them, and re-layouts: 7.6 us -> 2.59 us
    pallas_call x10 -> x11, Pallas kernels: 27 us -> 24.4 us  [call(): pl.pallas_call(kernel, out_shape=outs, in_specs=specs, out_specs=tuple((p...]
  transfers between devices with their start and end apart: 1 -> 2, of which waited for: 1 -> 2; matrix products, arithmetic and copies ran while one was open for 0% -> 0% of each run, Pallas kernels for 1% -> 1%
where the time goes in v2:
time: 182 us; the launch traced here: 181 us
  blocking collectives  119 us (65%)
  Pallas kernels  24.4 us (13%)
  waiting for transfers between devices  23 us (13%)
  starting transfers between devices  11.1 us (6%)
  local copies, waits for them, and re-layouts  2.59 us (1%)
    all_to_all x6, blocking collectives, exchange(): return lax.all_to_all(rows, ALL, split_axis=0, concat_axis=0, tiled=True)  119 us
    pallas_call x11, Pallas kernels, call(): pl.pallas_call(kernel, out_shape=outs, in_specs=specs, out_specs=tuple((p...  24.4 us
    all_to_all x2, waiting for transfers between devices, exchange(): return lax.all_to_all(rows, ALL, split_axis=0, concat_axis=0, tiled=True)  23 us
    all_to_all x2, starting transfers between devices, exchange(): return lax.all_to_all(rows, ALL, split_axis=0, concat_axis=0, tiled=True)  11.1 us
  transfers between devices with their start and end apart: 2, of which 2 were waited for; matrix products, arithmetic and copies ran while one was open for 0% of the time, Pallas kernels for 1%

profile of v2, /device:TPU:1, one launch (start us, length us, event | category | flops | bytes accessed | tf_op | source)
XLA Modules:
  0.0 181.2 jit_solution(11604199523833881531)
XLA Ops:
  0.6 2.6 %shard_map.103 = (f32[256,128]{1,0:T(8,128)}, f32[26,16,128]{2,1,0:T(8,128)}) custom-call(f32[3,4,4]{2,1,0:T(4,128)} %bitcast.53, s32[1,48]{1,0:T(1,128)} %bitcast.54, s32[4,4,128]{2,1,0:T(4,128)} %west_map.1, s32[4,4,128]{2,1,0:T(4,128)} %south_map.1, f32[4,3,4,512]{3,2,1,0:T(4,128)} %bitcast.52, f32[4,4,2,128]{3,2,1,0:T(2,128)} %load.1), custom_call_target="tpu_custom_call" | custom-call | tf_op jit(solution)/shard_map/pallas_call | solution.py:475
  3.3 28.4 %all_to_all.88 = f32[256,1,128]{2,1,0:T(1,128)S(1)} all-to-all(f32[256,1,128]{2,1,0:T(1,128)} %bitcast.51), channel_id=1, replica_groups=mesh['gx'=32,'gy'=8] {'gx','gy'}, dimensions={0} | all-to-all | bytes 262144 | tf_op jit(solution)/shard_map/all_to_all | solution.py:494
  31.7 0.0 copy-start
  31.7 1.7 copy-done
  33.4 0.0 copy-start.1
  33.4 1.5 shard_map.104
  34.9 5.5 %all-to-all-start.1 = ((f32[256,1,128]{2,1,0:T(1,128)}), f32[256,1,128]{2,1,0:T(1,128)S(1)}, u32[]{:S(2)}, u32[]{:S(2)}) async-start(f32[256,1,128]{2,1,0:T(1,128)} %bitcast.7), calls=%async_computation.1 | async-start | bytes 262144 | tf_op jit(solution)/shard_map/all_to_all | solution.py:494
  40.5 0.0 copy-start.2
  40.5 0.9 copy-done.2
  41.4 12.0 %all-to-all-done.1 = f32[256,1,128]{2,1,0:T(1,128)S(1)} async-done(((f32[256,1,128]{2,1,0:T(1,128)}), f32[256,1,128]{2,1,0:T(1,128)S(1)}, u32[]{:S(2)}, u32[]{:S(2)}) %all-to-all-start.1) | async-done | bytes 131104 | tf_op jit(solution)/shard_map/all_to_all | solution.py:494
  53.4 5.0 %shard_map.106 = (f32[256,128]{1,0:T(8,128)}, f32[8,16,128]{2,1,0:T(8,128)S(1)}, f32[40,16,128]{2,1,0:T(8,128)S(1)}) custom-call(f32[256,128]{1,0:T(8,128)S(1)} %bitcast.38, f32[26,16,128]{2,1,0:T(8,128)S(1)} %shard_map.105.kept, bf16[4,4,512,512]{3,2,1,0:T(8,128)(2,1)} %dual_ops.5), custom_call_target="tpu_custom_call" | custom-call | tf_op jit(solution)/shard_map/pallas_call | solution.py:475
  58.4 5.5 %all-to-all-start.2 = ((f32[256,1,128]{2,1,0:T(1,128)}), f32[256,1,128]{2,1,0:T(1,128)S(1)}, u32[]{:S(2)}, u32[]{:S(2)}) async-start(f32[256,1,128]{2,1,0:T(1,128)} %bitcast.10), calls=%async_computation.2 | async-start | bytes 262144 | tf_op jit(solution)/shard_map/all_to_all | solution.py:494
  63.9 1.9 %shard_map.107.owner = s32[256,128]{1,0:T(8,128)S(1)} custom-call(s32[256,128]{1,0:T(8,128)S(1)} %get-tuple-element.29.inverse), custom_call_target="tpu_custom_call" | custom-call | tf_op jit(solution)/shard_map/pallas_call | solution.py:475
  65.8 11.0 %all-to-all-done.2 = f32[256,1,128]{2,1,0:T(1,128)S(1)} async-done(((f32[256,1,128]{2,1,0:T(1,128)}), f32[256,1,128]{2,1,0:T(1,128)S(1)}, u32[]{:S(2)}, u32[]{:S(2)}) %all-to-all-start.2) | async-done | bytes 131104 | tf_op jit(solution)/shard_map/all_to_all | solution.py:494
  76.8 0.0 copy-done.1
  76.8 1.1 shard_map.108
  77.9 18.2 %all_to_all.89 = f32[256,1,128]{2,1,0:T(1,128)S(1)} all-to-all(f32[256,1,128]{2,1,0:T(1,128)S(1)} %bitcast.44), channel_id=1, replica_groups=mesh['gx'=32,'gy'=8] {'gx','gy'}, dimensions={0} | all-to-all | bytes 262144 | tf_op jit(solution)/shard_map/all_to_all | solution.py:494
  96.1 4.4 %shard_map.109 = (f32[256,128]{1,0:T(8,128)S(1)}, f32[13,16,128]{2,1,0:T(8,128)S(1)}) custom-call(f32[256,128]{1,0:T(8,128)S(1)} %bitcast.40, f32[40,16,128]{2,1,0:T(8,128)S(1)} %get-tuple-element.30.pack, bf16[4,4,512,512]{3,2,1,0:T(8,128)(2,1)} %dual_ops.5, f32[8,16,128]{2,1,0:T(8,128)S(1)} %get-tuple-element.31.before), custom_call_target="tpu_custom_call" | custom-call | tf_op jit(solution)/shard_map/pallas_call | solution.py:475
  100.5 18.3 %all_to_all.90 = f32[256,1,128]{2,1,0:T(1,128)S(1)} all-to-all(f32[256,1,128]{2,1,0:T(1,128)S(1)} %bitcast.48), channel_id=1, replica_groups=mesh['gx'=32,'gy'=8] {'gx','gy'}, dimensions={0} | all-to-all | bytes 262144 | tf_op jit(solution)/shard_map/all_to_all | solution.py:494
  118.8 1.1 shard_map.110
  119.9 18.2 %all_to_all.91 = f32[256,1,128]{2,1,0:T(1,128)S(1)} all-to-all(f32[256,1,128]{2,1,0:T(1,128)S(1)} %bitcast.50), channel_id=1, replica_groups=mesh['gx'=32,'gy'=8] {'gx','gy'}, dimensions={0} | all-to-all | bytes 262144 | tf_op jit(solution)/shard_map/all_to_all | solution.py:494
  138.0 4.6 %shard_map.111 = (f32[256,128]{1,0:T(8,128)S(1)}, f32[18,16,128]{2,1,0:T(8,128)S(1)}) custom-call(f32[256,128]{1,0:T(8,128)S(1)} %bitcast.39, f32[40,16,128]{2,1,0:T(8,128)S(1)} %get-tuple-element.30.pack, bf16[4,4,512,512]{3,2,1,0:T(8,128)(2,1)} %dual_ops.5, f32[13,16,128]{2,1,0:T(8,128)S(1)} %get-tuple-element.34.before, f32[1,128]{1,0:T(1,128)S(1)} %get-tuple-element.35.sums), custom_call_target="tpu_custom_call" | custom-call | tf_op jit(solution)/shard_map/pallas_call | solution.py:475
  142.7 18.2 %all_to_all.92 = f32[256,1,128]{2,1,0:T(1,128)S(1)} all-to-all(f32[256,1,128]{2,1,0:T(1,128)S(1)} %bitcast.49), channel_id=1, replica_groups=mesh['gx'=32,'gy'=8] {'gx','gy'}, dimensions={0} | all-to-all | bytes 262144 | tf_op jit(solution)/shard_map/all_to_all | solution.py:494
  160.8 1.1 shard_map.112
  161.9 18.2 %all_to_all.93 = f32[256,1,128]{2,1,0:T(1,128)S(1)} all-to-all(f32[256,1,128]{2,1,0:T(1,128)S(1)} %bitcast.47), channel_id=1, replica_groups=mesh['gx'=32,'gy'=8] {'gx','gy'}, dimensions={0} | all-to-all | bytes 262144 | tf_op jit(solution)/shard_map/all_to_all | solution.py:494
  180.0 1.1 shard_map.113
  (1 shorter events, 0.0 us)
Async XLA Ops:
  31.7 1.7 copy-start
  33.4 43.5 %copy-start.1 = (f32[48,12288]{1,0:T(8,128)S(1)}, f32[48,12288]{1,0:T(8,128)}, u32[]{:S(2)}) copy-start(f32[48,12288]{1,0:T(8,128)} %factor.7) | copy-start | bytes 7077892
  34.9 18.5 %all-to-all-start.1 = ((f32[256,1,128]{2,1,0:T(1,128)}), f32[256,1,128]{2,1,0:T(1,128)S(1)}, u32[]{:S(2)}, u32[]{:S(2)}) async-start(f32[256,1,128]{2,1,0:T(1,128)} %bitcast.7), calls=%async_computation.1 | async-start | bytes 262144 | tf_op jit(solution)/shard_map/all_to_all | solution.py:494
  40.5 0.9 copy-start.2
  58.4 18.5 %all-to-all-start.2 = ((f32[256,1,128]{2,1,0:T(1,128)}), f32[256,1,128]{2,1,0:T(1,128)S(1)}, u32[]{:S(2)}, u32[]{:S(2)}) async-start(f32[256,1,128]{2,1,0:T(1,128)} %bitcast.10), calls=%async_computation.2 | async-start | bytes 262144 | tf_op jit(solution)/shard_map/all_to_all | solution.py:494

commit v3 on v2

--- a/solution.py
+++ b/solution.py
@@ -149,6 +149,14 @@
     def times(self, k, left):
         self.copies[k].wait()
         return jnp.dot(left, self.held[k], preferred_element_type=jnp.float32)
+
+
+class Held:
+    def __init__(self, source):
+        self.source = source
+
+    def times(self, k, left):
+        return jnp.dot(left, self.source[k // 4, k % 4], preferred_element_type=jnp.float32)
 
 
 EDGE_ROWS = ([0, 1, 2, 3], [12, 13, 14, 15], [0, 4, 8, 12], [3, 7, 11, 15])
@@ -313,8 +321,8 @@
     state[LAM + 1] = u[3]
 
 
-def second_kernel(arrived, pack, dual_ops, before, out_row, state, *rest):
-    operators = Operators(dual_ops, *rest)
+def second_kernel(arrived, pack, dual_ops, before, out_row, state):
+    operators = Held(dual_ops)
     local = Local(pack)
     row = from_peers(arrived)
     _, image = image_of(local, arrived, before)
@@ -332,8 +340,8 @@
     state[COARSE] = jnp.broadcast_to(row, (SUB, LANES))
 
 
-def third_kernel(arrived, pack, dual_ops, before, sums, out_row, state, *rest):
-    operators = Operators(dual_ops, *rest)
+def third_kernel(arrived, pack, dual_ops, before, sums, out_row, state):
+    operators = Held(dual_ops)
     local = Local(pack)
     alpha = scalar(sums, 0) / scalar(sums, 1)
     row = from_peers(arrived)
@@ -482,8 +490,9 @@
     )(*args)
 
 
-def settle_kernel(value, out):
+def settle_kernel(value, inverse, out, owner):
     out[...] = value[...]
+    owner_kernel(inverse, owner)
 
 
 def after(first, *values):
@@ -510,8 +519,7 @@
     partial, inverse = call(coarse_first_kernel, (rows, indices), exchange(sent), coarse_factor)
     partial, (kept,) = after(partial, kept)
     arrived = exchange(partial)
-    (kept,) = call(settle_kernel, (f32(KEPT, SUB, E),), kept)
-    (owner,) = call(owner_kernel, (indices,), inverse)
+    kept, owner = call(settle_kernel, (f32(KEPT, SUB, E), indices), kept, inverse)
 
     def solve(sent, *sums):
         partial, *sums = call(coarse_kernel, (rows, *sums), exchange(sent), owner, inverse, coarse_factor)
@@ -522,11 +530,11 @@
     )
     (arrived,) = solve(sent)
     sent, state = call(
-        second_kernel, (rows, f32(13, SUB, E)), arrived, pack, dual_ops, state, operators=2
+        second_kernel, (rows, f32(13, SUB, E)), arrived, pack, dual_ops, state
     )
     arrived, sums = solve(sent, row)
     sent, state = call(
-        third_kernel, (rows, f32(18, SUB, E)), arrived, pack, dual_ops, state, sums, operators=2
+        third_kernel, (rows, f32(18, SUB, E)), arrived, pack, dual_ops, state, sums
     )
     arrived, sums_next = solve(sent, row)
     lam, gradient, amplitudes = call(

time: 182 us -> 175 us (0.962)
  blocking collectives: 119 us -> 138 us
  waiting for transfers between devices: 23 us -> 10.1 us
  Pallas kernels: 24.4 us -> 18.5 us
  starting transfers between devices: 11.1 us -> 5.53 us
    all_to_all x6 -> x7, blocking collectives: 119 us -> 138 us  [exchange(): return lax.all_to_all(rows, ALL, split_axis=0, concat_axis=0, tiled=True)]
    all_to_all x2 -> x1, waiting for transfers between devices: 23 us -> 10.1 us  [exchange(): return lax.all_to_all(rows, ALL, split_axis=0, concat_axis=0, tiled=True)]
    pallas_call x11 -> x10, Pallas kernels: 24.4 us -> 18.5 us  [call(): pl.pallas_call(kernel, out_shape=outs, in_specs=specs, out_specs=tuple((p...]
    all_to_all x2 -> x1, starting transfers between devices: 11.1 us -> 5.53 us  [exchange(): return lax.all_to_all(rows, ALL, split_axis=0, concat_axis=0, tiled=True)]
  transfers between devices with their start and end apart: 2 -> 1, of which waited for: 2 -> 1; matrix products, arithmetic and copies ran while one was open for 0% -> 0% of each run, Pallas kernels for 1% -> 1%
where the time goes in v3:
time: 175 us
  blocking collectives  138 us (79%)
  Pallas kernels  18.5 us (11%)
  waiting for transfers between devices  10.1 us (6%)
  starting transfers between devices  5.53 us (3%)
  local copies, waits for them, and re-layouts  2.6 us (1%)
    all_to_all x7, blocking collectives, exchange(): return lax.all_to_all(rows, ALL, split_axis=0, concat_axis=0, tiled=True)  138 us
    pallas_call x10, Pallas kernels, call(): pl.pallas_call(kernel, out_shape=outs, in_specs=specs, out_specs=tuple((p...  18.5 us
    all_to_all x1, waiting for transfers between devices, exchange(): return lax.all_to_all(rows, ALL, split_axis=0, concat_axis=0, tiled=True)  10.1 us
    all_to_all x1, starting transfers between devices, exchange(): return lax.all_to_all(rows, ALL, split_axis=0, concat_axis=0, tiled=True)  5.53 us
  transfers between devices with their start and end apart: 1, of which 1 were waited for; matrix products, arithmetic and copies ran while one was open for 0% of the time, Pallas kernels for 1%

profile of v3, /device:TPU:1, one launch (start us, length us, event | category | flops | bytes accessed | tf_op | source)
XLA Modules:
  0.0 175.0 jit_solution(14971284583500645701)
XLA Ops:
  0.6 2.6 %shard_map.103 = (f32[256,128]{1,0:T(8,128)}, f32[26,16,128]{2,1,0:T(8,128)}) custom-call(f32[3,4,4]{2,1,0:T(4,128)} %bitcast.54, s32[1,48]{1,0:T(1,128)} %bitcast.55, s32[4,4,128]{2,1,0:T(4,128)} %west_map.1, s32[4,4,128]{2,1,0:T(4,128)} %south_map.1, f32[4,3,4,512]{3,2,1,0:T(4,128)} %bitcast.53, f32[4,4,2,128]{3,2,1,0:T(2,128)} %load.1), custom_call_target="tpu_custom_call" | custom-call | tf_op jit(solution)/shard_map/pallas_call | solution.py:483
  3.3 28.4 %all_to_all.88 = f32[256,1,128]{2,1,0:T(1,128)S(1)} all-to-all(f32[256,1,128]{2,1,0:T(1,128)} %bitcast.52), channel_id=1, replica_groups=mesh['gx'=32,'gy'=8] {'gx','gy'}, dimensions={0} | all-to-all | bytes 262144 | tf_op jit(solution)/shard_map/all_to_all | solution.py:503
  31.7 0.0 copy-start.1
  31.7 1.7 copy-done.1
  33.4 0.0 copy-start.2
  33.4 1.5 shard_map.104
  34.9 5.5 %all-to-all-start.1 = ((f32[256,1,128]{2,1,0:T(1,128)}), f32[256,1,128]{2,1,0:T(1,128)S(1)}, u32[]{:S(2)}, u32[]{:S(2)}) async-start(f32[256,1,128]{2,1,0:T(1,128)} %bitcast.7), calls=%async_computation.1 | async-start | bytes 262144 | tf_op jit(solution)/shard_map/all_to_all | solution.py:503
  40.5 0.0 copy-start.3
  40.5 0.9 copy-done.3
  41.4 1.9 %shard_map.105 = (f32[26,16,128]{2,1,0:T(8,128)S(1)}, s32[256,128]{1,0:T(8,128)S(1)}) custom-call(f32[26,16,128]{2,1,0:T(8,128)S(1)} %copy-done.3, s32[256,128]{1,0:T(8,128)S(1)} %get-tuple-element.30.inverse), custom_call_target="tpu_custom_call" | custom-call | tf_op jit(solution)/shard_map/pallas_call | solution.py:483
  43.3 10.1 %all-to-all-done.1 = f32[256,1,128]{2,1,0:T(1,128)S(1)} async-done(((f32[256,1,128]{2,1,0:T(1,128)}), f32[256,1,128]{2,1,0:T(1,128)S(1)}, u32[]{:S(2)}, u32[]{:S(2)}) %all-to-all-start.1) | async-done | bytes 131104 | tf_op jit(solution)/shard_map/all_to_all | solution.py:503
  53.4 0.0 copy-start
  53.4 4.5 %shard_map.106 = (f32[256,128]{1,0:T(8,128)S(1)}, f32[8,16,128]{2,1,0:T(8,128)S(1)}, f32[40,16,128]{2,1,0:T(8,128)S(1)}) custom-call(f32[256,128]{1,0:T(8,128)S(1)} %bitcast.38, f32[26,16,128]{2,1,0:T(8,128)S(1)} %get-tuple-element.31.kept, bf16[4,4,512,512]{3,2,1,0:T(8,128)(2,1)} %dual_ops.5), custom_call_target="tpu_custom_call" | custom-call | tf_op jit(solution)/shard_map/pallas_call | solution.py:483
  57.9 18.3 %all_to_all.89 = f32[256,1,128]{2,1,0:T(1,128)S(1)} all-to-all(f32[256,1,128]{2,1,0:T(1,128)S(1)} %bitcast.47), channel_id=1, replica_groups=mesh['gx'=32,'gy'=8] {'gx','gy'}, dimensions={0} | all-to-all | bytes 262144 | tf_op jit(solution)/shard_map/all_to_all | solution.py:503
  76.2 0.0 copy-done.2
  76.2 1.1 shard_map.107
  77.3 18.2 %all_to_all.90 = f32[256,1,128]{2,1,0:T(1,128)S(1)} all-to-all(f32[256,1,128]{2,1,0:T(1,128)S(1)} %bitcast.44), channel_id=1, replica_groups=mesh['gx'=32,'gy'=8] {'gx','gy'}, dimensions={0} | all-to-all | bytes 262144 | tf_op jit(solution)/shard_map/all_to_all | solution.py:503
  95.4 0.0 copy-done
  95.4 1.6 shard_map.108
  97.1 18.2 %all_to_all.91 = f32[256,1,128]{2,1,0:T(1,128)S(1)} all-to-all(f32[256,1,128]{2,1,0:T(1,128)S(1)} %bitcast.49), channel_id=1, replica_groups=mesh['gx'=32,'gy'=8] {'gx','gy'}, dimensions={0} | all-to-all | bytes 262144 | tf_op jit(solution)/shard_map/all_to_all | solution.py:503
  115.2 1.1 shard_map.109
  116.3 18.2 %all_to_all.92 = f32[256,1,128]{2,1,0:T(1,128)S(1)} all-to-all(f32[256,1,128]{2,1,0:T(1,128)S(1)} %bitcast.51), channel_id=1, replica_groups=mesh['gx'=32,'gy'=8] {'gx','gy'}, dimensions={0} | all-to-all | bytes 262144 | tf_op jit(solution)/shard_map/all_to_all | solution.py:503
  134.5 2.0 %shard_map.110 = (f32[256,128]{1,0:T(8,128)S(1)}, f32[18,16,128]{2,1,0:T(8,128)S(1)}) custom-call(f32[256,128]{1,0:T(8,128)S(1)} %bitcast.39, f32[40,16,128]{2,1,0:T(8,128)S(1)} %get-tuple-element.34.pack, bf16[4,4,512,512]{3,2,1,0:T(8,128)(2,1)S(1)} %copy-done, f32[13,16,128]{2,1,0:T(8,128)S(1)} %get-tuple-element.38.before, ...), custom_call_target="tpu_custom_call" | custom-call | tf_op jit(solution)/shard_map/pallas_call | solution.py:483
  136.5 18.2 %all_to_all.93 = f32[256,1,128]{2,1,0:T(1,128)S(1)} all-to-all(f32[256,1,128]{2,1,0:T(1,128)S(1)} %bitcast.50), channel_id=1, replica_groups=mesh['gx'=32,'gy'=8] {'gx','gy'}, dimensions={0} | all-to-all | bytes 262144 | tf_op jit(solution)/shard_map/all_to_all | solution.py:503
  154.6 1.1 shard_map.111
  155.7 18.2 %all_to_all.94 = f32[256,1,128]{2,1,0:T(1,128)S(1)} all-to-all(f32[256,1,128]{2,1,0:T(1,128)S(1)} %bitcast.48), channel_id=1, replica_groups=mesh['gx'=32,'gy'=8] {'gx','gy'}, dimensions={0} | all-to-all | bytes 262144 | tf_op jit(solution)/shard_map/all_to_all | solution.py:503
  173.9 1.1 shard_map.112
Async XLA Ops:
  31.7 1.7 copy-start.1
  33.4 42.8 %copy-start.2 = (f32[48,12288]{1,0:T(8,128)S(1)}, f32[48,12288]{1,0:T(8,128)}, u32[]{:S(2)}) copy-start(f32[48,12288]{1,0:T(8,128)} %factor.7) | copy-start | bytes 7077892
  34.9 18.5 %all-to-all-start.1 = ((f32[256,1,128]{2,1,0:T(1,128)}), f32[256,1,128]{2,1,0:T(1,128)S(1)}, u32[]{:S(2)}, u32[]{:S(2)}) async-start(f32[256,1,128]{2,1,0:T(1,128)} %bitcast.7), calls=%async_computation.1 | async-start | bytes 262144 | tf_op jit(solution)/shard_map/all_to_all | solution.py:503
  40.5 0.9 copy-start.3
  53.4 42.1 %copy-start = (bf16[4,4,512,512]{3,2,1,0:T(8,128)(2,1)S(1)}, bf16[4,4,512,512]{3,2,1,0:T(8,128)(2,1)}, u32[]{:S(2)}) copy-start(bf16[4,4,512,512]{3,2,1,0:T(8,128)(2,1)} %dual_ops.5) | copy-start | bytes 25165828

commit v4 on v3

--- a/solution.py
+++ b/solution.py
@@ -129,6 +129,7 @@
             if precise:
                 product = product[:SUB] + product[SUB:]
             out = jnp.where(row == k, product, out)
+        out = operators.finish(out)
         w = [out[:, side * E : (side + 1) * E] for side in range(4)]
         t = lane_gather(w[0], self.maps[WINV]), lane_gather(w[2], self.maps[SINV])
         return w, t
@@ -137,18 +138,38 @@
         send_rows(jnp.sum(total, axis=0, keepdims=True), edges, ref)
 
 
+HALF = 2 * E
+
+
 class Operators:
-    def __init__(self, source, held, arrived):
-        self.held = held
+    def __init__(self, source, top, low, arrived):
+        self.top, self.low = top, low
         self.copies = []
+        self.mirrored = jnp.zeros((HALF, LANES), jnp.float32)
+        first, rest = pl.ds(0, HALF), pl.ds(HALF, HALF)
         for k in range(SUB):
-            copy = pltpu.make_async_copy(source.at[k // 4, k % 4], held.at[k], arrived.at[k])
-            copy.start()
-            self.copies.append(copy)
+            whole = source.at[k // 4, k % 4]
+            for i, (part, held) in enumerate(((whole.at[first], top), (whole.at[rest, rest], low))):
+                copy = pltpu.make_async_copy(part, held.at[k], arrived.at[i, k])
+                copy.start()
+                self.copies.append(copy)
 
     def times(self, k, left):
-        self.copies[k].wait()
-        return jnp.dot(left, self.held[k], preferred_element_type=jnp.float32)
+        for copy in self.copies[2 * k : 2 * k + 2]:
+            copy.wait()
+        first, rest = left[:, :HALF], left[:, HALF:]
+        if k == 0:
+            filled = jnp.concatenate([rest.astype(jnp.float32), jnp.zeros((LANES - SUB, HALF), jnp.float32)], axis=0)
+            self.columns = filled.T.astype(jnp.bfloat16)
+        dot = lambda a, b: jnp.dot(a, b, preferred_element_type=jnp.float32)
+        beside = self.top[k, :, HALF:]
+        lane = lax.broadcasted_iota(jnp.int32, (HALF, LANES), 1)
+        self.mirrored = jnp.where(lane == k, dot(beside, self.columns), self.mirrored)
+        lower = dot(first, beside) + dot(rest, self.low[k])
+        return jnp.concatenate([dot(first, self.top[k, :, :HALF]), lower], axis=1)
+
+    def finish(self, out):
+        return jnp.concatenate([out[:, :HALF] + self.mirrored.T[:SUB], out[:, HALF:]], axis=1)
 
 
 class Held:
@@ -157,6 +178,9 @@
 
     def times(self, k, left):
         return jnp.dot(left, self.source[k // 4, k % 4], preferred_element_type=jnp.float32)
+
+    def finish(self, out):
+        return out
 
 
 EDGE_ROWS = ([0, 1, 2, 3], [12, 13, 14, 15], [0, 4, 8, 12], [3, 7, 11, 15])
@@ -477,8 +501,9 @@
     if operators is not None:
         megabytes = 50
         scratch = [
-            pltpu.VMEM((SUB, 4 * E, 4 * E), jnp.bfloat16),
-            pltpu.SemaphoreType.DMA((SUB,)),
+            pltpu.VMEM((SUB, HALF, 4 * E), jnp.bfloat16),
+            pltpu.VMEM((SUB, HALF, HALF), jnp.bfloat16),
+            pltpu.SemaphoreType.DMA((2, SUB)),
         ]
     return pl.pallas_call(
         kernel,

time: 175 us -> 176 us (level)
  no operation moved by 1% of the time
where the time goes in v4:
time: 176 us
  blocking collectives  138 us (78%)
  Pallas kernels  19.2 us (11%)
  waiting for transfers between devices  10.1 us (6%)
  starting transfers between devices  5.53 us (3%)
  local copies, waits for them, and re-layouts  2.6 us (1%)
    all_to_all x7, blocking collectives, exchange(): return lax.all_to_all(rows, ALL, split_axis=0, concat_axis=0, tiled=True)  138 us
    pallas_call x10, Pallas kernels, call(): pl.pallas_call(kernel, out_shape=outs, in_specs=specs, out_specs=tuple((p...  19.2 us
    all_to_all x1, waiting for transfers between devices, exchange(): return lax.all_to_all(rows, ALL, split_axis=0, concat_axis=0, tiled=True)  10.1 us
    all_to_all x1, starting transfers between devices, exchange(): return lax.all_to_all(rows, ALL, split_axis=0, concat_axis=0, tiled=True)  5.53 us
  transfers between devices with their start and end apart: 1, of which 1 were waited for; matrix products, arithmetic and copies ran while one was open for 0% of the time, Pallas kernels for 1%

profile of v4, /device:TPU:1, one launch (start us, length us, event | category | flops | bytes accessed | tf_op | source)
XLA Modules:
  0.0 175.7 jit_solution(11715975930624375195)
XLA Ops:
  0.6 2.6 %shard_map.103 = (f32[256,128]{1,0:T(8,128)}, f32[26,16,128]{2,1,0:T(8,128)}) custom-call(f32[3,4,4]{2,1,0:T(4,128)} %bitcast.54, s32[1,48]{1,0:T(1,128)} %bitcast.55, s32[4,4,128]{2,1,0:T(4,128)} %west_map.1, s32[4,4,128]{2,1,0:T(4,128)} %south_map.1, f32[4,3,4,512]{3,2,1,0:T(4,128)} %bitcast.53, f32[4,4,2,128]{3,2,1,0:T(2,128)} %load.1), custom_call_target="tpu_custom_call" | custom-call | tf_op jit(solution)/shard_map/pallas_call | solution.py:508
  3.3 28.4 %all_to_all.88 = f32[256,1,128]{2,1,0:T(1,128)S(1)} all-to-all(f32[256,1,128]{2,1,0:T(1,128)} %bitcast.52), channel_id=1, replica_groups=mesh['gx'=32,'gy'=8] {'gx','gy'}, dimensions={0} | all-to-all | bytes 262144 | tf_op jit(solution)/shard_map/all_to_all | solution.py:528
  31.7 0.0 copy-start.1
  31.7 1.7 copy-done.1
  33.4 0.0 copy-start.2
  33.4 1.5 shard_map.104
  34.9 5.5 %all-to-all-start.1 = ((f32[256,1,128]{2,1,0:T(1,128)}), f32[256,1,128]{2,1,0:T(1,128)S(1)}, u32[]{:S(2)}, u32[]{:S(2)}) async-start(f32[256,1,128]{2,1,0:T(1,128)} %bitcast.7), calls=%async_computation.1 | async-start | bytes 262144 | tf_op jit(solution)/shard_map/all_to_all | solution.py:528
  40.5 0.0 copy-start.3
  40.5 0.9 copy-done.3
  41.4 1.9 %shard_map.105 = (f32[26,16,128]{2,1,0:T(8,128)S(1)}, s32[256,128]{1,0:T(8,128)S(1)}) custom-call(f32[26,16,128]{2,1,0:T(8,128)S(1)} %copy-done.3, s32[256,128]{1,0:T(8,128)S(1)} %get-tuple-element.30.inverse), custom_call_target="tpu_custom_call" | custom-call | tf_op jit(solution)/shard_map/pallas_call | solution.py:508
  43.3 10.1 %all-to-all-done.1 = f32[256,1,128]{2,1,0:T(1,128)S(1)} async-done(((f32[256,1,128]{2,1,0:T(1,128)}), f32[256,1,128]{2,1,0:T(1,128)S(1)}, u32[]{:S(2)}, u32[]{:S(2)}) %all-to-all-start.1) | async-done | bytes 131104 | tf_op jit(solution)/shard_map/all_to_all | solution.py:528
  53.4 0.0 copy-start
  53.4 5.2 %shard_map.106 = (f32[256,128]{1,0:T(8,128)S(1)}, f32[8,16,128]{2,1,0:T(8,128)S(1)}, f32[40,16,128]{2,1,0:T(8,128)S(1)}) custom-call(f32[256,128]{1,0:T(8,128)S(1)} %bitcast.38, f32[26,16,128]{2,1,0:T(8,128)S(1)} %get-tuple-element.31.kept, bf16[4,4,512,512]{3,2,1,0:T(8,128)(2,1)} %dual_ops.5), custom_call_target="tpu_custom_call" | custom-call | tf_op jit(solution)/shard_map/pallas_call | solution.py:508
  58.6 18.2 %all_to_all.89 = f32[256,1,128]{2,1,0:T(1,128)S(1)} all-to-all(f32[256,1,128]{2,1,0:T(1,128)S(1)} %bitcast.47), channel_id=1, replica_groups=mesh['gx'=32,'gy'=8] {'gx','gy'}, dimensions={0} | all-to-all | bytes 262144 | tf_op jit(solution)/shard_map/all_to_all | solution.py:528
  76.7 0.0 copy-done.2
  76.7 1.1 shard_map.107
  77.8 18.3 %all_to_all.90 = f32[256,1,128]{2,1,0:T(1,128)S(1)} all-to-all(f32[256,1,128]{2,1,0:T(1,128)S(1)} %bitcast.44), channel_id=1, replica_groups=mesh['gx'=32,'gy'=8] {'gx','gy'}, dimensions={0} | all-to-all | bytes 262144 | tf_op jit(solution)/shard_map/all_to_all | solution.py:528
  96.1 0.0 copy-done
  96.1 1.6 shard_map.108
  97.8 18.2 %all_to_all.91 = f32[256,1,128]{2,1,0:T(1,128)S(1)} all-to-all(f32[256,1,128]{2,1,0:T(1,128)S(1)} %bitcast.49), channel_id=1, replica_groups=mesh['gx'=32,'gy'=8] {'gx','gy'}, dimensions={0} | all-to-all | bytes 262144 | tf_op jit(solution)/shard_map/all_to_all | solution.py:528
  116.0 1.1 shard_map.109
  117.0 18.2 %all_to_all.92 = f32[256,1,128]{2,1,0:T(1,128)S(1)} all-to-all(f32[256,1,128]{2,1,0:T(1,128)S(1)} %bitcast.51), channel_id=1, replica_groups=mesh['gx'=32,'gy'=8] {'gx','gy'}, dimensions={0} | all-to-all | bytes 262144 | tf_op jit(solution)/shard_map/all_to_all | solution.py:528
  135.2 2.0 %shard_map.110 = (f32[256,128]{1,0:T(8,128)S(1)}, f32[18,16,128]{2,1,0:T(8,128)S(1)}) custom-call(f32[256,128]{1,0:T(8,128)S(1)} %bitcast.39, f32[40,16,128]{2,1,0:T(8,128)S(1)} %get-tuple-element.34.pack, bf16[4,4,512,512]{3,2,1,0:T(8,128)(2,1)S(1)} %copy-done, f32[13,16,128]{2,1,0:T(8,128)S(1)} %get-tuple-element.38.before, ...), custom_call_target="tpu_custom_call" | custom-call | tf_op jit(solution)/shard_map/pallas_call | solution.py:508
  137.2 18.2 %all_to_all.93 = f32[256,1,128]{2,1,0:T(1,128)S(1)} all-to-all(f32[256,1,128]{2,1,0:T(1,128)S(1)} %bitcast.50), channel_id=1, replica_groups=mesh['gx'=32,'gy'=8] {'gx','gy'}, dimensions={0} | all-to-all | bytes 262144 | tf_op jit(solution)/shard_map/all_to_all | solution.py:528
  155.3 1.1 shard_map.111
  156.4 18.2 %all_to_all.94 = f32[256,1,128]{2,1,0:T(1,128)S(1)} all-to-all(f32[256,1,128]{2,1,0:T(1,128)S(1)} %bitcast.48), channel_id=1, replica_groups=mesh['gx'=32,'gy'=8] {'gx','gy'}, dimensions={0} | all-to-all | bytes 262144 | tf_op jit(solution)/shard_map/all_to_all | solution.py:528
  174.6 1.1 shard_map.112
Async XLA Ops:
  31.7 1.7 copy-start.1
  33.4 43.4 %copy-start.2 = (f32[48,12288]{1,0:T(8,128)S(1)}, f32[48,12288]{1,0:T(8,128)}, u32[]{:S(2)}) copy-start(f32[48,12288]{1,0:T(8,128)} %factor.7) | copy-start | bytes 7077892
  34.9 18.5 %all-to-all-start.1 = ((f32[256,1,128]{2,1,0:T(1,128)}), f32[256,1,128]{2,1,0:T(1,128)S(1)}, u32[]{:S(2)}, u32[]{:S(2)}) async-start(f32[256,1,128]{2,1,0:T(1,128)} %bitcast.7), calls=%async_computation.1 | async-start | bytes 262144 | tf_op jit(solution)/shard_map/all_to_all | solution.py:528
  40.5 0.9 copy-start.3
  53.4 42.8 %copy-start = (bf16[4,4,512,512]{3,2,1,0:T(8,128)(2,1)S(1)}, bf16[4,4,512,512]{3,2,1,0:T(8,128)(2,1)}, u32[]{:S(2)}) copy-start(bf16[4,4,512,512]{3,2,1,0:T(8,128)(2,1)} %dual_ops.5) | copy-start | bytes 25165828
